TPU v7x, 32 devices: a whole 2x2x4 slice. The times are simulated.
32 devices in a mesh: groups: 1, expert: 16 (over z, y, core), req: 2 (over x).
Axes of the slice: x: 2, y: 2, z: 4, core: 2. Of those that a mesh axis runs over, the one named last changes fastest.
Arguments:
- tree_hidden: bfloat16 [512, 3584], P(('groups', 'expert', 'req')), may hold values from -6 to 6
- expert_ids: int32 [512, 8], P(('groups', 'expert', 'req')), may hold values from 0 to 15, all different within a row; in each aligned block of 16 rows (0 to 15, 16 to 31, ...) at most 16 rows name the same one
- route_weights: float32 [512, 8], P(('groups', 'expert', 'req')), may hold values from 0.1 to 1
- w_up: bfloat16 [16, 3584, 1024], P('expert', None, 'req'), may hold values from -0.09375 to 0.09375
- w_down: bfloat16 [16, 1024, 3584], P('expert', None, 'req'), may hold values from -0.1875 to 0.1875
- accept_count: int32 [32], P(('groups', 'expert', 'req')), may hold values from 1 to 8
- accept_pos: int32 [32, 8], P(('groups', 'expert', 'req')), may hold values from 0 to 15, as said below
- draft_owner: int32 [32], P(('groups', 'expert', 'req')), may hold values from 0 to 1, as said below
- mtp_gain: float32 [3584], replicated, may hold values from 0.5 to 1.5
Outputs:
- layer_out: bfloat16 [512, 3584], P(('groups', 'expert', 'req'))
- draft_inputs: bfloat16 [32, 8, 3584], P(('groups', 'expert', 'req'))
Inputs may be any that keep to these rules, and one draw needn't show every extreme that they name: `expert_ids`: in the rows of one device each expert is named by at most 16 rows. `accept_pos`: each row holds distinct tree positions in increasing order. `draft_owner`: the requests q with the same q // 2 have distinct owners.
All inputs are finite; a program needn't handle non-finite values.
Results may differ from a plain program's by a relative error of at most 0.0057.
Values may be sent and summed in bfloat16 or wider, within the bound.
No kernel may reach another device: no remote copies, remote signals or barrier semaphores. Data moves between devices by JAX's collectives and lax.ppermute only.
A program may use at most 64 MiB of HBM per device.

v0:
```python
import jax
import jax.numpy as jnp
from jax import lax
from jax.sharding import PartitionSpec as P


def find_slots(route_ids, expert_count):
    flat_ids = route_ids.reshape(-1)
    matches = (flat_ids[:, None] == jnp.arange(expert_count, dtype=jnp.int32)[None, :]).astype(
        jnp.int32
    )
    earlier = jnp.cumsum(matches, axis=0) - matches
    return jnp.sum(earlier * matches, axis=1).reshape(route_ids.shape)


def send_matrix(target, length):
    places = jnp.arange(length, dtype=jnp.int32)
    return jnp.any(places[:, None, None] == target[None, :, :], axis=2).astype(jnp.bfloat16)


def local(
    tree_hidden,
    expert_ids,
    route_weights,
    w_up,
    w_down,
    accept_count,
    accept_pos,
    draft_owner,
    mtp_gain,
):
    expert_count = lax.axis_size("expert")
    req_count = lax.axis_size("req")
    tree_len, top_k = expert_ids.shape
    capacity = min(tree_len, max(4, 2 * tree_len * top_k // expert_count))
    up_local = w_up[0]
    down_local = w_down[0]
    own_target = expert_ids * capacity + find_slots(expert_ids, expert_count)
    mapping = send_matrix(own_target, expert_count * capacity)
    outgoing = jnp.dot(mapping, tree_hidden, preferred_element_type=jnp.float32).astype(
        jnp.bfloat16
    )
    outgoing = outgoing.reshape(expert_count, capacity, -1)
    arrived = lax.all_to_all(outgoing, "expert", split_axis=0, concat_axis=0, tiled=True)
    activated = jax.nn.silu(
        jnp.dot(
            lax.all_gather(arrived.reshape(expert_count * capacity, -1), "req", axis=0, tiled=True),
            up_local,
            preferred_element_type=jnp.float32,
        )
    ).astype(jnp.bfloat16)
    produced = jnp.dot(
        lax.all_gather(activated, "req", axis=1, tiled=True),
        down_local,
        preferred_element_type=jnp.float32,
    ).astype(jnp.bfloat16)
    shaped = produced.reshape(req_count, expert_count, capacity, -1)
    returned = lax.all_to_all(
        lax.all_to_all(shaped, "expert", split_axis=1, concat_axis=1, tiled=True),
        "req",
        split_axis=0,
        concat_axis=3,
        tiled=True,
    )
    returned = returned.reshape(expert_count * capacity, -1)
    places = jnp.arange(expert_count * capacity, dtype=jnp.int32)
    combine = jnp.sum(
        jnp.where(own_target[:, :, None] == places[None, None, :], route_weights[:, :, None], 0.0),
        axis=1,
    )
    mixed = jnp.dot(combine, returned.astype(jnp.float32), precision=lax.Precision.HIGHEST)
    layer_local = (tree_hidden.astype(jnp.float32) + mixed).astype(jnp.bfloat16)
    accept_len = accept_pos.shape[1]
    position_hit = accept_pos[0][:, None] == jnp.arange(tree_len, dtype=jnp.int32)[None, :]
    live = jnp.arange(accept_len, dtype=jnp.int32)[:, None] < accept_count[0]
    selector = (position_hit & live).astype(jnp.bfloat16)
    accepted = jnp.dot(selector, layer_local, preferred_element_type=jnp.float32).astype(
        jnp.bfloat16
    )
    owner_mask = (jnp.arange(req_count, dtype=jnp.int32) == draft_owner[0])[:, None, None]
    parcel = jnp.where(owner_mask, accepted[None], jnp.zeros_like(accepted)[None])
    delivered = lax.all_to_all(parcel, "req", split_axis=0, concat_axis=0, tiled=True)
    incoming = jnp.sum(delivered.astype(jnp.float32), axis=0)
    scale = lax.rsqrt(jnp.mean(incoming * incoming, axis=-1, keepdims=True) + 1e-06)
    draft_local = (incoming * scale * mtp_gain[None, :]).astype(jnp.bfloat16)[None]
    return (layer_local, draft_local)


def solution(mesh):
    return jax.shard_map(
        local,
        mesh=mesh,
        in_specs=(
            P(("groups", "expert", "req"), None),
            P(("groups", "expert", "req"), None),
            P(("groups", "expert", "req"), None),
            P("expert", None, "req"),
            P("expert", None, "req"),
            P(("groups", "expert", "req")),
            P(("groups", "expert", "req"), None),
            P(("groups", "expert", "req")),
            P(),
        ),
        out_specs=(
            P(("groups", "expert", "req"), None),
            P(("groups", "expert", "req"), None, None),
        ),
        check_vma=False,
    )
```

profile of v0, /device:TPU:0, one launch (start us, length us, event | category | flops | bytes accessed | tf_op | source)
XLA Modules:
  0.0 237.2 jit_solution(5424743455922961028)
XLA Ops:
  7.2 0.0 all-gather.3.cloned.1.call-start
  7.2 0.8 copy.28
  8.0 0.1 eq.66
  8.1 0.1 fusion.13
  8.2 0.2 reduce_window_sum.11
  8.3 0.2 select_reduce_fusion.1
  8.5 0.1 reshape.97
  8.6 0.1 fusion.10
  8.7 1.6 convolution_convert_fusion
  10.3 50.0 %all_to_all.30 = bf16[16,16,3584]{2,1,0:T(8,128)(2,1)} all-to-all(bf16[16,16,3584]{2,1,0:T(8,128)(2,1)S(1)} %bitcast.41), channel_id=1, replica_groups=mesh['groups'=1,'expert'=16,'req'=2] {'expert'}, dimensions={0} | all-to-all | bytes 3670016 | tf_op jit(solution)/shard_map/all_to_all | solution.py:44
  60.4 0.0 all-gather.3.cloned.1.call-update
  60.4 0.0 all-gather.5.cloned.1.call-start
  60.4 50.3 %all-gather.3.cloned.1.call-done = bf16[512,3584]{1,0:T(8,128)(2,1)} async-done(((bf16[256,3584]{1,0:T(8,128)(2,1)}), bf16[512,3584]{1,0:T(8,128)(2,1)}) %all-gather.3.cloned.1.call-update) | async-done | bytes 3670032 | tf_op jit(solution)/shard_map/all_gather | solution.py:47
  110.7 6.2 %multiply_convert_fusion = bf16[512,512]{1,0:T(8,128)(2,1)} fusion(bf16[512,3584]{1,0:T(8,128)(2,1)} %all-gather.3.cloned.1.call-done, bf16[1,3584,512]{2,1,0:T(8,128)(2,1)} %param.12), kind=kOutput, calls=%fused_computation.9 | convolution fusion | flops 1880358912 | bytes 7864320 | tf_op jit(solution)/shard_map/dot_general | solution.py:46
  116.9 0.0 all-gather.5.cloned.1.call-update
  116.9 21.5 %all-gather.5.cloned.1.call-done = bf16[512,1024]{1,0:T(8,128)(2,1)} async-done(((bf16[512,512]{1,0:T(8,128)(2,1)}), bf16[512,1024]{1,0:T(8,128)(2,1)}) %all-gather.5.cloned.1.call-update) | async-done | bytes 1048592 | tf_op jit(solution)/shard_map/all_gather | solution.py:53
  138.4 4.4 %fusion.5 = bf16[512,1792]{1,0:T(8,128)(2,1)S(1)} fusion(bf16[512,1024]{1,0:T(8,128)(2,1)} %all-gather.5.cloned.1.call-done, bf16[1,1024,1792]{2,1,0:T(8,128)(2,1)} %param.13), kind=kOutput, calls=%fused_computation.8 | convolution fusion | flops 1879965696 | bytes 6553600 | tf_op jit(solution)/shard_map/dot_general | solution.py:52
  142.8 0.2 copy.31
  143.0 48.2 %all_to_all.31 = bf16[2,16,16,1792]{3,2,0,1:T(8,128)(2,1)S(1)} all-to-all(bf16[2,16,16,1792]{3,2,0,1:T(8,128)(2,1)S(1)} %copy.31), channel_id=1, replica_groups=mesh['groups'=1,'expert'=16,'req'=2] {'expert'}, dimensions={1} | all-to-all | bytes 3670016 | tf_op jit(solution)/shard_map/all_to_all | solution.py:59
  191.2 1.4 copy.32
  192.6 3.7 %all-to-all-start.2 = ((bf16[2,16,16,1792]{3,2,1,0:T(8,128)(2,1)}), bf16[2,16,16,1792]{3,2,1,0:T(8,128)(2,1)S(1)}, u32[]{:S(2)}, u32[]{:S(2)}) async-start(bf16[2,16,16,1792]{3,2,1,0:T(8,128)(2,1)} %copy.32), calls=%async_computation.2 | async-start | bytes 3670016 | tf_op jit(solution)/shard_map/all_to_all | solution.py:58
  196.3 0.1 copy.30
  197.7 0.1 select_reduce_fusion
  197.8 21.7 %all-to-all-done.2 = bf16[2,16,16,1792]{3,2,1,0:T(8,128)(2,1)S(1)} async-done(((bf16[2,16,16,1792]{3,2,1,0:T(8,128)(2,1)}), bf16[2,16,16,1792]{3,2,1,0:T(8,128)(2,1)S(1)}, u32[]{:S(2)}, u32[]{:S(2)}) %all-to-all-start.2) | async-done | bytes 1835040 | tf_op jit(solution)/shard_map/all_to_all | solution.py:58
  219.5 1.9 copy.33
  221.4 0.2 copy.34
  221.6 0.8 fusion
  222.5 0.2 convolution_convert_fusion.1
  222.7 0.1 broadcast_select_fusion
  222.8 6.8 %all_to_all.32 = bf16[2,8,3584]{2,1,0:T(8,128)(2,1)S(1)} all-to-all(bf16[2,8,3584]{2,1,0:T(8,128)(2,1)S(1)} %broadcast_select_fusion), channel_id=1, replica_groups=mesh['groups'=1,'expert'=16,'req'=2] {'req'}, dimensions={0} | all-to-all | bytes 229376 | tf_op jit(solution)/shard_map/all_to_all | solution.py:82
  229.5 0.1 multiply_reduce_fusion
  229.7 0.7 fusion.12
  (15 shorter events, 0.1 us)
Async XLA Ops:
  7.2 103.5 %all-gather.3.cloned.1.call-start = ((), (), s32[]{:S(2)}) async-start(), calls=%async_computation.4 | async-start | bytes 5505024 | tf_op jit(solution)/shard_map/all_gather | solution.py:47
  60.4 78.0 %all-gather.5.cloned.1.call-start = ((), (), s32[]{:S(2)}) async-start(), calls=%async_computation.5 | async-start | bytes 1572864 | tf_op jit(solution)/shard_map/all_gather | solution.py:53
  191.2 5.1 %copy-start.3 = (f32[16,8]{0,1:T(8,128)S(1)}, f32[16,8]{0,1:T(8,128)}, u32[]{:S(2)}) copy-start(f32[16,8]{0,1:T(8,128)} %param.11) | copy-start | bytes 1540
  192.6 26.9 %all-to-all-start.2 = ((bf16[2,16,16,1792]{3,2,1,0:T(8,128)(2,1)}), bf16[2,16,16,1792]{3,2,1,0:T(8,128)(2,1)S(1)}, u32[]{:S(2)}, u32[]{:S(2)}) async-start(bf16[2,16,16,1792]{3,2,1,0:T(8,128)(2,1)} %copy.32), calls=%async_computation.2 | async-start | bytes 3670016 | tf_op jit(solution)/shard_map/all_to_all | solution.py:58
  219.5 2.1 copy-start.1
  221.4 1.1 copy-start.4
  221.4 8.3 %copy-start.2 = (f32[3584]{0:T(1024)S(1)}, f32[3584]{0:T(1024)}, u32[]{:S(2)}) copy-start(f32[3584]{0:T(1024)} %param.17) | copy-start | bytes 43012
  222.5 7.9 %copy-start = (bf16[16,3584]{1,0:T(8,128)(2,1)}, bf16[16,3584]{1,0:T(8,128)(2,1)S(1)}, u32[]{:S(2)}) copy-start(bf16[16,3584]{1,0:T(8,128)(2,1)S(1)} %fusion) | copy-start | bytes 344068
Sparse Core Ops, SparseCore 0:
  60.5 50.1 all-gather.2
  117.0 21.2 all-gather.4
where the time goes:
time: 238 us; the launch traced here: 237 us
  blocking collectives  105 us (44%)
  waiting for transfers between devices  93.4 us (39%)
  between operations  15.5 us (7%)
  matrix products  13.2 us (6%)
  local copies, waits for them, and re-layouts  4.69 us (2%)
  starting transfers between devices  3.8 us (2%)
    all_gather x1, waiting for transfers between devices, local(): lax.all_gather(arrived.reshape(expert_count * capacity, -1), 'req', axis=...  50.3 us
    all_to_all x1, blocking collectives, local(): lax.all_to_all(outgoing, 'expert', split_axis=0, concat_axis=0, tiled=True)  50 us
    all_to_all x1, blocking collectives, local(): lax.all_to_all(shaped, 'expert', split_axis=1, concat_axis=1, tiled=True)  48.2 us
    all_to_all x1, waiting for transfers between devices, local(): lax.all_to_all(lax.all_to_all(shaped, 'expert', split_axis=1, concat_axis...  21.7 us
    all_gather x1, waiting for transfers between devices, local(): lax.all_gather(activated, 'req', axis=1, tiled=True)  21.5 us
    all_to_all x1, blocking collectives, local(): lax.all_to_all(parcel, 'req', split_axis=0, concat_axis=0, tiled=True)  6.75 us
    dot_general x1, matrix products, local(): jnp.dot(lax.all_gather(arrived.reshape(expert_count * capacity, -1), 'req...  6.17 us
  transfers between devices with their start and end apart: 3, of which 3 were waited for; matrix products, arithmetic and copies ran while one was open for 0% of the time, Pallas kernels for 0%

commit v1 on v0

--- a/solution.py
+++ b/solution.py
@@ -18,7 +18,11 @@
     return jnp.any(places[:, None, None] == target[None, :, :], axis=2).astype(jnp.bfloat16)
 
 
-def local(
+def capacity_of(tree_len, top_k, expert_count):
+    return min(tree_len, max(4, 2 * tree_len * top_k // expert_count))
+
+
+def routed_plan(
     tree_hidden,
     expert_ids,
     route_weights,
@@ -32,7 +36,7 @@
     expert_count = lax.axis_size("expert")
     req_count = lax.axis_size("req")
     tree_len, top_k = expert_ids.shape
-    capacity = min(tree_len, max(4, 2 * tree_len * top_k // expert_count))
+    capacity = capacity_of(tree_len, top_k, expert_count)
     up_local = w_up[0]
     down_local = w_down[0]
     own_target = expert_ids * capacity + find_slots(expert_ids, expert_count)
@@ -70,10 +74,7 @@
     )
     mixed = jnp.dot(combine, returned.astype(jnp.float32), precision=lax.Precision.HIGHEST)
     layer_local = (tree_hidden.astype(jnp.float32) + mixed).astype(jnp.bfloat16)
-    accept_len = accept_pos.shape[1]
-    position_hit = accept_pos[0][:, None] == jnp.arange(tree_len, dtype=jnp.int32)[None, :]
-    live = jnp.arange(accept_len, dtype=jnp.int32)[:, None] < accept_count[0]
-    selector = (position_hit & live).astype(jnp.bfloat16)
+    selector = selector_of(accept_pos, accept_count, tree_len)
     accepted = jnp.dot(selector, layer_local, preferred_element_type=jnp.float32).astype(
         jnp.bfloat16
     )
@@ -81,12 +82,152 @@
     parcel = jnp.where(owner_mask, accepted[None], jnp.zeros_like(accepted)[None])
     delivered = lax.all_to_all(parcel, "req", split_axis=0, concat_axis=0, tiled=True)
     incoming = jnp.sum(delivered.astype(jnp.float32), axis=0)
-    scale = lax.rsqrt(jnp.mean(incoming * incoming, axis=-1, keepdims=True) + 1e-06)
-    draft_local = (incoming * scale * mtp_gain[None, :]).astype(jnp.bfloat16)[None]
-    return (layer_local, draft_local)
+    return (layer_local, norm_rows(incoming, mtp_gain))
+
+
+def selector_of(accept_pos, accept_count, tree_len):
+    accept_len = accept_pos.shape[1]
+    position_hit = accept_pos[0][:, None] == jnp.arange(tree_len, dtype=jnp.int32)[None, :]
+    live = jnp.arange(accept_len, dtype=jnp.int32)[:, None] < accept_count[0]
+    return (position_hit & live).astype(jnp.bfloat16)
+
+
+def norm_rows(rows, gain):
+    scale = lax.rsqrt(jnp.mean(rows * rows, axis=-1, keepdims=True) + 1e-06)
+    return (rows * scale * gain[None, :]).astype(jnp.bfloat16)[None]
+
+
+def swap(array, axis, bit):
+    size = lax.axis_size(axis)
+    return lax.ppermute(array, axis, [(i, i ^ bit) for i in range(size)])
+
+
+def three_parts(value):
+    first = value.astype(jnp.bfloat16)
+    rest = value - first.astype(jnp.float32)
+    second = rest.astype(jnp.bfloat16)
+    third = (rest - second.astype(jnp.float32)).astype(jnp.bfloat16)
+    return [first, second, third]
+
+
+CORE, Y, NEAR, FAR = ("expert", 1), ("expert", 2), ("expert", 4), ("expert", 8)
+X = ("req", 1)
+
+
+def gather(block, steps):
+    for axis, bit in steps:
+        block = jnp.concatenate([block, swap(block, axis, bit)], axis=0)
+    return block
+
+
+def gathered_plan(
+    tree_hidden,
+    expert_ids,
+    route_weights,
+    w_up,
+    w_down,
+    accept_count,
+    accept_pos,
+    draft_owner,
+    mtp_gain,
+):
+    expert_count = lax.axis_size("expert")
+    tree_len, features = tree_hidden.shape
+    accept_len = accept_pos.shape[1]
+    me = lax.axis_index("expert")
+    side = lax.axis_index("req")
+    hidden_half = w_up.shape[2]
+    feature_half = w_down.shape[2]
+    half = tree_len // 2
+
+    w_own = lax.dynamic_slice_in_dim(w_down[0], side * hidden_half, hidden_half, 0)
+    w_other = lax.dynamic_slice_in_dim(w_down[0], (1 - side) * hidden_half, hidden_half, 0)
+
+    experts = jnp.arange(expert_count, dtype=jnp.int32)
+    dense = jnp.sum(
+        jnp.where(expert_ids[:, :, None] == experts[None, None, :], route_weights[:, :, None], 0.0),
+        axis=1,
+    )
+    selector = selector_of(accept_pos, accept_count, tree_len)
+    selector = jnp.pad(selector, ((0, tree_len - accept_len), (0, 0)))
+    extra = jnp.concatenate(three_parts(dense) + [selector], axis=1)
+    extra = jnp.pad(extra, ((0, 0), (0, -extra.shape[1] % 128)))
+    rows = jnp.concatenate([tree_hidden, extra], axis=1)
+
+    steps = [(FAR, NEAR, Y, X, CORE), (FAR, NEAR, X, Y, CORE)]
+    blocks = [gather(rows[k * half : (k + 1) * half], steps[k]) for k in range(2)]
+
+    here = (experts == me).astype(jnp.float32)
+    own, weight = [], []
+    for k in range(2):
+        own.append(
+            jax.nn.silu(
+                jnp.dot(blocks[k][:, :features], w_up[0], preferred_element_type=jnp.float32)
+            ).astype(jnp.bfloat16)
+        )
+        parts = blocks[k][:, features:].astype(jnp.float32)
+        total = sum(parts[:, j * expert_count : (j + 1) * expert_count] for j in range(3))
+        weight.append(jnp.sum(total * here[None, :], axis=1, keepdims=True))
+    other = []
+    for k in range(2):
+        below = 1 << steps[k].index(X)
+        turned = own[k].reshape(-1, 2, below * half, hidden_half)[:, ::-1]
+        other.append(swap(turned.reshape(own[k].shape), *X))
+    sums = []
+    for k in range(2):
+        produced = jnp.dot(own[k], w_own, preferred_element_type=jnp.float32) + jnp.dot(
+            other[k], w_other, preferred_element_type=jnp.float32
+        )
+        sums.append(produced.astype(jnp.bfloat16).astype(jnp.float32) * weight[k])
+
+    back = [(CORE, Y, NEAR, FAR), (CORE, NEAR, Y, FAR)]
+    done = []
+    for k in range(2):
+        names = list(reversed(steps[k]))
+        total = sums[k].reshape((2,) * len(names) + (half, feature_half))
+        for step in back[k]:
+            at = names.index(step)
+            keep = lax.index_in_dim(total, 0, at, keepdims=False)
+            send = lax.index_in_dim(total, 1, at, keepdims=False).astype(jnp.bfloat16)
+            shape = keep.shape
+            received = swap(send.reshape(-1, feature_half), *step).reshape(shape)
+            total = keep + received.astype(jnp.float32)
+            names.remove(step)
+        done.append(total)
+    mixed = jnp.concatenate(done, axis=1)
+
+    place = [len(set(steps[k][: steps[k].index(X)])) for k in range(2)]
+    second = jnp.concatenate(
+        [blocks[k][half << place[k] : (half << place[k]) + half] for k in range(2)], axis=0
+    )
+    pair_hidden = jnp.stack([tree_hidden, second[:, :features]])
+    pair_part = lax.dynamic_slice_in_dim(pair_hidden, side * feature_half, feature_half, 2)
+    layer_part = (pair_part.astype(jnp.float32) + mixed).astype(jnp.bfloat16)
+    received = swap(layer_part.reshape(2 * tree_len, feature_half), *X)
+    received = received.reshape(2, tree_len, feature_half)[::-1]
+    layer_pair = jnp.where(
+        side == 0,
+        jnp.concatenate([layer_part, received], axis=2),
+        jnp.concatenate([received, layer_part], axis=2),
+    )
+    layer_local = layer_pair[0]
+    at = features + 3 * expert_count
+    stays = draft_owner[0] == side
+    chosen = jnp.where(stays, layer_local, layer_pair[1])
+    chosen_selector = jnp.where(stays, rows[:accept_len, at : at + tree_len], second[:accept_len, at : at + tree_len])
+    incoming = jnp.dot(chosen_selector, chosen, preferred_element_type=jnp.float32)
+    return (layer_local, norm_rows(incoming, mtp_gain))
 
 
 def solution(mesh):
+    def local(*arrays):
+        tree_len, top_k = arrays[1].shape
+        expert_count = mesh.shape["expert"]
+        whole = capacity_of(tree_len, top_k, expert_count) == tree_len
+        if whole and expert_count == 16 and mesh.shape["req"] == 2:
+            return gathered_plan(*arrays)
+        return routed_plan(*arrays)
+
     return jax.shard_map(
         local,
         mesh=mesh,

time: 238 us -> 87.2 us (0.37)
  blocking collectives: 105 us -> 0 us
  waiting for transfers between devices: 93.4 us -> 37.2 us
  starting transfers between devices: 3.8 us -> 29.5 us
  between operations: 15.5 us -> 2.31 us
  matrix products: 13.2 us -> 6.98 us
  local copies, waits for them, and re-layouts: 4.69 us -> 7.58 us
    all_to_all x3 -> x0, blocking collectives: 105 us -> none  [the longest x1 50 us: local(): lax.all_to_all(outgoing, 'expert', split_axis=0, concat_axis=0, tiled=True)]
    all_gather x2 -> x0, waiting for transfers between devices: 71.7 us -> none  [the longest x1 50.3 us: local(): lax.all_gather(arrived.reshape(expert_count * capacity, -1), 'req', axis=...]
    ppermute x0 -> x21, waiting for transfers between devices: none -> 37.2 us  [swap(): return lax.ppermute(array, axis, [(i, i ^ bit) for i in range(size)])]
    ppermute x0 -> x21, starting transfers between devices: none -> 29.5 us  [swap(): return lax.ppermute(array, axis, [(i, i ^ bit) for i in range(size)])]
    all_to_all x1 -> x0, waiting for transfers between devices: 21.7 us -> none  [local(): lax.all_to_all(lax.all_to_all(shaped, 'expert', split_axis=1, concat_axis...]
    dot_general x5 -> x7, matrix products: 13.2 us -> 6.98 us  [the longest x2 2.94 us: gathered_plan(): jnp.dot(own[k], w_own, preferred_element_type=jnp.float32)]
    unnamed x13 -> x23, local copies, waits for them, and re-layouts: 1.05 us -> 6.13 us
    all_to_all x1 -> x0, starting transfers between devices: 3.72 us -> none  [local(): lax.all_to_all(lax.all_to_all(shaped, 'expert', split_axis=1, concat_axis...]
  transfers between devices with their start and end apart: 3 -> 21, of which waited for: 3 -> 17; matrix products, arithmetic and copies ran while one was open for 0% -> 13% of each run, Pallas kernels for 0% -> 0%
where the time goes in v1:
time: 87.2 us; the launch traced here: 87 us
  waiting for transfers between devices  37.2 us (43%)
  starting transfers between devices  29.5 us (34%)
  local copies, waits for them, and re-layouts  7.58 us (9%)
  matrix products  6.98 us (8%)
  other arithmetic  3.48 us (4%)
  between operations  2.31 us (3%)
    ppermute x21, waiting for transfers between devices, swap(): return lax.ppermute(array, axis, [(i, i ^ bit) for i in range(size)])  37.2 us
    ppermute x21, starting transfers between devices, swap(): return lax.ppermute(array, axis, [(i, i ^ bit) for i in range(size)])  29.5 us
    unnamed x23, local copies, waits for them, and re-layouts  6.13 us
    dot_general x2, matrix products, gathered_plan(): jnp.dot(own[k], w_own, preferred_element_type=jnp.float32)  2.94 us
    dot_general x2, matrix products, gathered_plan(): jnp.dot(blocks[k][:, :features], w_up[0], preferred_element_type=jnp.floa...  2.39 us
  transfers between devices with their start and end apart: 21, of which 17 were waited for; matrix products, arithmetic and copies ran while one was open for 13% of the time, Pallas kernels for 0%

profile of v1, /device:TPU:0, one launch (start us, length us, event | category | flops | bytes accessed | tf_op | source)
XLA Modules:
  0.0 87.0 jit_solution(1929147507108465118)
XLA Ops:
  3.7 0.9 %fusion.40 = bf16[16,3712]{1,0:T(8,128)(2,1)S(1)} fusion(bf16[16,64]{1,0:T(8,128)(2,1)S(1)} %fusion.54, bf16[16,3584]{1,0:T(8,128)(2,1)} %param.9), kind=kLoop, calls=%fused_computation.61 | loop fusion | flops 356352 | bytes 235520 | tf_op jit(solution)/shard_map/concatenate | solution.py:155
  5.3 4.0 %collective-permute-start = (bf16[8,3712]{1,0:T(8,128)(2,1)S(1)}, bf16[8,3712]{1,0:T(8,128)(2,1)S(1)}, u32[]{:S(2)}, u32[]{:S(2)}) collective-permute-start(bf16[8,3712]{1,0:T(8,128)(2,1)S(1)} %get-tuple-element.19), channel_id=1, source_target_pairs={{0,16},{2,18},{4,20},{6,22},{8,24},{10,26},{12,28},{14,30},{16,0},... | collective-permute-start | bytes 178184 | tf_op jit(solution)/shard_map/ppermute | solution.py:102
  9.4 2.8 %collective-permute-done = bf16[8,3712]{1,0:T(8,128)(2,1)S(1)} collective-permute-done((bf16[8,3712]{1,0:T(8,128)(2,1)S(1)}, bf16[8,3712]{1,0:T(8,128)(2,1)S(1)}, u32[]{:S(2)}, u32[]{:S(2)}) %collective-permute-start) | collective-permute-done | bytes 59424 | tf_op jit(solution)/shard_map/ppermute | solution.py:102
  12.2 2.6 %collective-permute-start.1 = (bf16[16,3712]{1,0:T(8,128)(2,1)S(1)}, bf16[16,3712]{1,0:T(8,128)(2,1)S(1)}, u32[]{:S(2)}, u32[]{:S(2)}) collective-permute-start(bf16[16,3712]{1,0:T(8,128)(2,1)S(1)} %pad_maximum_fusion.4), channel_id=1, source_target_pairs={{0,8},{2,10},{4,12},{6,14},{8,0},{10,2},{12,4},{14,6},{16,24},{18,... | collective-permute-start | bytes 356360 | tf_op jit(solution)/shard_map/ppermute | solution.py:102
  14.8 1.3 %collective-permute-start.5 = (bf16[16,3712]{1,0:T(8,128)(2,1)S(1)}, bf16[16,3712]{1,0:T(8,128)(2,1)S(1)}, u32[]{:S(2)}, u32[]{:S(2)}) collective-permute-start(bf16[16,3712]{1,0:T(8,128)(2,1)S(1)} %pad_maximum_fusion.5), channel_id=1, source_target_pairs={{0,8},{2,10},{4,12},{6,14},{8,0},{10,2},{12,4},{14,6},{16,24},{18,... | collective-permute-start | bytes 356360 | tf_op jit(solution)/shard_map/ppermute | solution.py:102
  17.4 1.4 %collective-permute-done.1 = bf16[16,3712]{1,0:T(8,128)(2,1)S(1)} collective-permute-done((bf16[16,3712]{1,0:T(8,128)(2,1)S(1)}, bf16[16,3712]{1,0:T(8,128)(2,1)S(1)}, u32[]{:S(2)}, u32[]{:S(2)}) %collective-permute-start.1) | collective-permute-done | bytes 118816 | tf_op jit(solution)/shard_map/ppermute | solution.py:102
  18.8 1.7 %collective-permute-start.2 = (bf16[32,3712]{1,0:T(8,128)(2,1)S(1)}, bf16[32,3712]{1,0:T(8,128)(2,1)S(1)}, u32[]{:S(2)}, u32[]{:S(2)}) collective-permute-start(bf16[32,3712]{1,0:T(8,128)(2,1)S(1)} %pad_maximum_fusion.2), channel_id=1, source_target_pairs={{0,4},{2,6},{4,0},{6,2},{8,12},{10,14},{12,8},{14,10},{16,20},{18,... | collective-permute-start | bytes 712712 | tf_op jit(solution)/shard_map/ppermute | solution.py:102
  20.7 1.6 %collective-permute-start.6 = (bf16[32,3712]{1,0:T(8,128)(2,1)S(1)}, bf16[32,3712]{1,0:T(8,128)(2,1)S(1)}, u32[]{:S(2)}, u32[]{:S(2)}) collective-permute-start(bf16[32,3712]{1,0:T(8,128)(2,1)S(1)} %pad_maximum_fusion.3), channel_id=1, source_target_pairs={{0,1},{1,0},{2,3},{3,2},{4,5},{5,4},{6,7},{7,6},{8,9},{9,8},{10,11... | collective-permute-start | bytes 712712 | tf_op jit(solution)/shard_map/ppermute | solution.py:102
  23.5 1.7 %collective-permute-done.2 = bf16[32,3712]{1,0:T(8,128)(2,1)S(1)} collective-permute-done((bf16[32,3712]{1,0:T(8,128)(2,1)S(1)}, bf16[32,3712]{1,0:T(8,128)(2,1)S(1)}, u32[]{:S(2)}, u32[]{:S(2)}) %collective-permute-start.2) | collective-permute-done | bytes 237600 | tf_op jit(solution)/shard_map/ppermute | solution.py:102
  25.3 1.5 %collective-permute-start.3 = (bf16[64,3712]{1,0:T(8,128)(2,1)S(1)}, bf16[64,3712]{1,0:T(8,128)(2,1)S(1)}, u32[]{:S(2)}, u32[]{:S(2)}) collective-permute-start(bf16[64,3712]{1,0:T(8,128)(2,1)S(1)} %pad_maximum_fusion), channel_id=1, source_target_pairs={{0,1},{1,0},{2,3},{3,2},{4,5},{5,4},{6,7},{7,6},{8,9},{9,8},{10,11... | collective-permute-start | bytes 1425416 | tf_op jit(solution)/shard_map/ppermute | solution.py:102
  26.8 2.7 %collective-permute-done.6 = bf16[32,3712]{1,0:T(8,128)(2,1)S(1)} collective-permute-done((bf16[32,3712]{1,0:T(8,128)(2,1)S(1)}, bf16[32,3712]{1,0:T(8,128)(2,1)S(1)}, u32[]{:S(2)}, u32[]{:S(2)}) %collective-permute-start.6) | collective-permute-done | bytes 237600 | tf_op jit(solution)/shard_map/ppermute | solution.py:102
  29.5 1.6 %collective-permute-start.13 = (bf16[64,3712]{1,0:T(8,128)(2,1)S(1)}, bf16[64,3712]{1,0:T(8,128)(2,1)S(1)}, u32[]{:S(2)}, u32[]{:S(2)}) collective-permute-start(bf16[64,3712]{1,0:T(8,128)(2,1)S(1)} %pad_maximum_fusion.1), channel_id=1, source_target_pairs={{0,4},{2,6},{4,0},{6,2},{8,12},{10,14},{12,8},{14,10},{16,20},{18,... | collective-permute-start | bytes 1425416 | tf_op jit(solution)/shard_map/ppermute | solution.py:102
  31.1 6.9 %collective-permute-done.3 = bf16[64,3712]{1,0:T(8,128)(2,1)S(1)} collective-permute-done((bf16[64,3712]{1,0:T(8,128)(2,1)S(1)}, bf16[64,3712]{1,0:T(8,128)(2,1)S(1)}, u32[]{:S(2)}, u32[]{:S(2)}) %collective-permute-start.3) | collective-permute-done | bytes 475168 | tf_op jit(solution)/shard_map/ppermute | solution.py:102
  39.1 0.8 constant_dynamic-update-slice_fusion.11
  41.3 1.2 %multiply_convert_fusion.1 = bf16[256,512]{1,0:T(8,128)(2,1)S(1)} fusion(bf16[1,3584,512]{2,1,0:T(8,128)(2,1)S(1)} %copy-done.6, bf16[256,3712]{1,0:T(8,128)(2,1)S(1)} %constant_dynamic-update-slice_fusion.5), kind=kOutput, calls=%fused_computation.29 | convolution fusion | flops 940179456 | bytes 5767168 | tf_op jit(solution)/shard_map/dot_general | solution.py:165
  42.9 1.2 %multiply_convert_fusion = bf16[256,512]{1,0:T(8,128)(2,1)S(1)} fusion(bf16[1,3584,512]{2,1,0:T(8,128)(2,1)S(1)} %copy-done.6, bf16[256,3712]{1,0:T(8,128)(2,1)S(1)} %constant_dynamic-update-slice_fusion.16), kind=kOutput, calls=%fused_computation.28 | convolution fusion | flops 940179456 | bytes 5767168 | tf_op jit(solution)/shard_map/dot_general | solution.py:165
  44.1 1.3 %collective-permute-start.8 = (bf16[256,512]{1,0:T(8,128)(2,1)S(1)}, bf16[256,512]{1,0:T(8,128)(2,1)S(1)}, u32[]{:S(2)}, u32[]{:S(2)}) collective-permute-start(bf16[256,512]{1,0:T(8,128)(2,1)S(1)} %bitcast.105), channel_id=1, source_target_pairs={{0,1},{1,0},{2,3},{3,2},{4,5},{5,4},{6,7},{7,6},{8,9},{9,8},{10,11... | collective-permute-start | bytes 786440 | tf_op jit(solution)/shard_map/ppermute | solution.py:102
  45.4 0.8 collective-permute-start.15
  46.6 2.3 %fusion.16 = f32[256,1792]{1,0:T(8,128)S(1)} fusion(bf16[256,512]{1,0:T(8,128)(2,1)S(1)} %multiply_convert_fusion.1, bf16[1,1024,1792]{2,1,0:T(8,128)(2,1)} %param.13, s32[]{:T(128)S(6)} %select_n.40), kind=kOutput, calls=%fused_computation.18 | convolution fusion | flops 469762048 | bytes 3932164 | tf_op jit(solution)/shard_map/dot_general | solution.py:178
  48.9 4.4 %collective-permute-done.8 = bf16[256,512]{1,0:T(8,128)(2,1)S(1)} collective-permute-done((bf16[256,512]{1,0:T(8,128)(2,1)S(1)}, bf16[256,512]{1,0:T(8,128)(2,1)S(1)}, u32[]{:S(2)}, u32[]{:S(2)}) %collective-permute-start.8) | collective-permute-done | bytes 262176 | tf_op jit(solution)/shard_map/ppermute | solution.py:102
  54.7 3.5 %collective-permute-done.15 = bf16[256,512]{1,0:T(8,128)(2,1)S(1)} collective-permute-done((bf16[256,512]{1,0:T(8,128)(2,1)S(1)}, bf16[256,512]{1,0:T(8,128)(2,1)S(1)}, u32[]{:S(2)}, u32[]{:S(2)}) %collective-permute-start.15) | collective-permute-done | bytes 262176 | tf_op jit(solution)/shard_map/ppermute | solution.py:102
  59.2 1.4 %collective-permute-start.10 = (bf16[64,1792]{1,0:T(8,128)(2,1)S(1)}, bf16[64,1792]{1,0:T(8,128)(2,1)S(1)}, u32[]{:S(2)}, u32[]{:S(2)}) collective-permute-start(bf16[64,1792]{1,0:T(8,128)(2,1)S(1)} %bitcast.107), channel_id=1, source_target_pairs={{0,4},{2,6},{4,0},{6,2},{8,12},{10,14},{12,8},{14,10},{16,20},{18,... | collective-permute-start | bytes 688136 | tf_op jit(solution)/shard_map/ppermute | solution.py:102
  61.0 1.5 %collective-permute-start.17 = (bf16[64,1792]{1,0:T(8,128)(2,1)S(1)}, bf16[64,1792]{1,0:T(8,128)(2,1)S(1)}, u32[]{:S(2)}, u32[]{:S(2)}) collective-permute-start(bf16[64,1792]{1,0:T(8,128)(2,1)S(1)} %bitcast.106), channel_id=1, source_target_pairs={{0,8},{2,10},{4,12},{6,14},{8,0},{10,2},{12,4},{14,6},{16,24},{18,... | collective-permute-start | bytes 688136 | tf_op jit(solution)/shard_map/ppermute | solution.py:102
  62.5 4.8 %collective-permute-done.10 = bf16[64,1792]{1,0:T(8,128)(2,1)S(1)} collective-permute-done((bf16[64,1792]{1,0:T(8,128)(2,1)S(1)}, bf16[64,1792]{1,0:T(8,128)(2,1)S(1)}, u32[]{:S(2)}, u32[]{:S(2)}) %collective-permute-start.10) | collective-permute-done | bytes 229408 | tf_op jit(solution)/shard_map/ppermute | solution.py:102
  67.3 1.5 %collective-permute-start.11 = (bf16[32,1792]{1,0:T(8,128)(2,1)S(1)}, bf16[32,1792]{1,0:T(8,128)(2,1)S(1)}, u32[]{:S(2)}, u32[]{:S(2)}) collective-permute-start(bf16[32,1792]{1,0:T(8,128)(2,1)S(1)} %bitcast.110), channel_id=1, source_target_pairs={{0,8},{2,10},{4,12},{6,14},{8,0},{10,2},{12,4},{14,6},{16,24},{18,... | collective-permute-start | bytes 344072 | tf_op jit(solution)/shard_map/ppermute | solution.py:102
  68.9 1.6 %collective-permute-start.18 = (bf16[32,1792]{1,0:T(8,128)(2,1)S(1)}, bf16[32,1792]{1,0:T(8,128)(2,1)S(1)}, u32[]{:S(2)}, u32[]{:S(2)}) collective-permute-start(bf16[32,1792]{1,0:T(8,128)(2,1)S(1)} %bitcast.111), channel_id=1, source_target_pairs={{0,4},{2,6},{4,0},{6,2},{8,12},{10,14},{12,8},{14,10},{16,20},{18,... | collective-permute-start | bytes 344072 | tf_op jit(solution)/shard_map/ppermute | solution.py:102
  70.5 1.7 %collective-permute-done.11 = bf16[32,1792]{1,0:T(8,128)(2,1)S(1)} collective-permute-done((bf16[32,1792]{1,0:T(8,128)(2,1)S(1)}, bf16[32,1792]{1,0:T(8,128)(2,1)S(1)}, u32[]{:S(2)}, u32[]{:S(2)}) %collective-permute-start.11) | collective-permute-done | bytes 114720 | tf_op jit(solution)/shard_map/ppermute | solution.py:102
  72.2 3.4 %collective-permute-start.12 = (bf16[16,1792]{1,0:T(8,128)(2,1)S(1)}, bf16[16,1792]{1,0:T(8,128)(2,1)S(1)}, u32[]{:S(2)}, u32[]{:S(2)}) collective-permute-start(bf16[16,1792]{1,0:T(8,128)(2,1)S(1)} %fusion.50), channel_id=1, source_target_pairs={{0,16},{2,18},{4,20},{6,22},{8,24},{10,26},{12,28},{14,30},{16,0},... | collective-permute-start | bytes 172040 | tf_op jit(solution)/shard_map/ppermute | solution.py:102
  75.7 1.6 %collective-permute-start.19 = (bf16[16,1792]{1,0:T(8,128)(2,1)S(1)}, bf16[16,1792]{1,0:T(8,128)(2,1)S(1)}, u32[]{:S(2)}, u32[]{:S(2)}) collective-permute-start(bf16[16,1792]{1,0:T(8,128)(2,1)S(1)} %fusion.51), channel_id=1, source_target_pairs={{0,16},{2,18},{4,20},{6,22},{8,24},{10,26},{12,28},{14,30},{16,0},... | collective-permute-start | bytes 172040 | tf_op jit(solution)/shard_map/ppermute | solution.py:102
  78.1 2.7 %collective-permute-done.19 = bf16[16,1792]{1,0:T(8,128)(2,1)S(1)} collective-permute-done((bf16[16,1792]{1,0:T(8,128)(2,1)S(1)}, bf16[16,1792]{1,0:T(8,128)(2,1)S(1)}, u32[]{:S(2)}, u32[]{:S(2)}) %collective-permute-start.19) | collective-permute-done | bytes 57376 | tf_op jit(solution)/shard_map/ppermute | solution.py:102
  80.9 1.6 %collective-permute-start.20 = (bf16[32,1792]{1,0:T(8,128)(2,1)S(1)}, bf16[32,1792]{1,0:T(8,128)(2,1)S(1)}, u32[]{:S(2)}, u32[]{:S(2)}) collective-permute-start(bf16[32,1792]{1,0:T(8,128)(2,1)S(1)} %bitcast.103), channel_id=1, source_target_pairs={{0,1},{1,0},{2,3},{3,2},{4,5},{5,4},{6,7},{7,6},{8,9},{9,8},{10,11... | collective-permute-start | bytes 344072 | tf_op jit(solution)/shard_map/ppermute | solution.py:102
  83.1 2.6 %collective-permute-done.20 = bf16[32,1792]{1,0:T(8,128)(2,1)S(1)} collective-permute-done((bf16[32,1792]{1,0:T(8,128)(2,1)S(1)}, bf16[32,1792]{1,0:T(8,128)(2,1)S(1)}, u32[]{:S(2)}, u32[]{:S(2)}) %collective-permute-start.20) | collective-permute-done | bytes 114720 | tf_op jit(solution)/shard_map/ppermute | solution.py:102
  (89 shorter events, 14.1 us)
Async XLA Ops:
  5.3 6.8 %collective-permute-start = (bf16[8,3712]{1,0:T(8,128)(2,1)S(1)}, bf16[8,3712]{1,0:T(8,128)(2,1)S(1)}, u32[]{:S(2)}, u32[]{:S(2)}) collective-permute-start(bf16[8,3712]{1,0:T(8,128)(2,1)S(1)} %get-tuple-element.19), channel_id=1, source_target_pairs={{0,16},{2,18},{4,20},{6,22},{8,24},{10,26},{12,28},{14,30},{16,0},... | collective-permute-start | bytes 178184 | tf_op jit(solution)/shard_map/ppermute | solution.py:102
  9.4 5.4 %collective-permute-start.4 = (bf16[8,3712]{1,0:T(8,128)(2,1)S(1)}, bf16[8,3712]{1,0:T(8,128)(2,1)S(1)}, u32[]{:S(2)}, u32[]{:S(2)}) collective-permute-start(bf16[8,3712]{1,0:T(8,128)(2,1)S(1)} %get-tuple-element.18), channel_id=1, source_target_pairs={{0,16},{2,18},{4,20},{6,22},{8,24},{10,26},{12,28},{14,30},{16,0},... | collective-permute-start | bytes 178184 | tf_op jit(solution)/shard_map/ppermute | solution.py:102
  12.2 6.6 %collective-permute-start.1 = (bf16[16,3712]{1,0:T(8,128)(2,1)S(1)}, bf16[16,3712]{1,0:T(8,128)(2,1)S(1)}, u32[]{:S(2)}, u32[]{:S(2)}) collective-permute-start(bf16[16,3712]{1,0:T(8,128)(2,1)S(1)} %pad_maximum_fusion.4), channel_id=1, source_target_pairs={{0,8},{2,10},{4,12},{6,14},{8,0},{10,2},{12,4},{14,6},{16,24},{18,... | collective-permute-start | bytes 356360 | tf_op jit(solution)/shard_map/ppermute | solution.py:102
  14.8 5.8 %collective-permute-start.5 = (bf16[16,3712]{1,0:T(8,128)(2,1)S(1)}, bf16[16,3712]{1,0:T(8,128)(2,1)S(1)}, u32[]{:S(2)}, u32[]{:S(2)}) collective-permute-start(bf16[16,3712]{1,0:T(8,128)(2,1)S(1)} %pad_maximum_fusion.5), channel_id=1, source_target_pairs={{0,8},{2,10},{4,12},{6,14},{8,0},{10,2},{12,4},{14,6},{16,24},{18,... | collective-permute-start | bytes 356360 | tf_op jit(solution)/shard_map/ppermute | solution.py:102
  18.8 6.4 %collective-permute-start.2 = (bf16[32,3712]{1,0:T(8,128)(2,1)S(1)}, bf16[32,3712]{1,0:T(8,128)(2,1)S(1)}, u32[]{:S(2)}, u32[]{:S(2)}) collective-permute-start(bf16[32,3712]{1,0:T(8,128)(2,1)S(1)} %pad_maximum_fusion.2), channel_id=1, source_target_pairs={{0,4},{2,6},{4,0},{6,2},{8,12},{10,14},{12,8},{14,10},{16,20},{18,... | collective-permute-start | bytes 712712 | tf_op jit(solution)/shard_map/ppermute | solution.py:102
  20.7 8.8 %collective-permute-start.6 = (bf16[32,3712]{1,0:T(8,128)(2,1)S(1)}, bf16[32,3712]{1,0:T(8,128)(2,1)S(1)}, u32[]{:S(2)}, u32[]{:S(2)}) collective-permute-start(bf16[32,3712]{1,0:T(8,128)(2,1)S(1)} %pad_maximum_fusion.3), channel_id=1, source_target_pairs={{0,1},{1,0},{2,3},{3,2},{4,5},{5,4},{6,7},{7,6},{8,9},{9,8},{10,11... | collective-permute-start | bytes 712712 | tf_op jit(solution)/shard_map/ppermute | solution.py:102
  22.9 8.2 %copy-start.4 = (bf16[256,3712]{1,0:T(8,128)(2,1)S(1)}, bf16[256,3712]{1,0:T(8,128)(2,1)}, u32[]{:S(2)}) copy-start(bf16[256,3712]{1,0:T(8,128)(2,1)} %get-tuple-element.13) | copy-start | bytes 5701636
  25.3 12.7 %collective-permute-start.3 = (bf16[64,3712]{1,0:T(8,128)(2,1)S(1)}, bf16[64,3712]{1,0:T(8,128)(2,1)S(1)}, u32[]{:S(2)}, u32[]{:S(2)}) collective-permute-start(bf16[64,3712]{1,0:T(8,128)(2,1)S(1)} %pad_maximum_fusion), channel_id=1, source_target_pairs={{0,1},{1,0},{2,3},{3,2},{4,5},{5,4},{6,7},{7,6},{8,9},{9,8},{10,11... | collective-permute-start | bytes 1425416 | tf_op jit(solution)/shard_map/ppermute | solution.py:102
  29.5 9.6 %collective-permute-start.13 = (bf16[64,3712]{1,0:T(8,128)(2,1)S(1)}, bf16[64,3712]{1,0:T(8,128)(2,1)S(1)}, u32[]{:S(2)}, u32[]{:S(2)}) collective-permute-start(bf16[64,3712]{1,0:T(8,128)(2,1)S(1)} %pad_maximum_fusion.1), channel_id=1, source_target_pairs={{0,4},{2,6},{4,0},{6,2},{8,12},{10,14},{12,8},{14,10},{16,20},{18,... | collective-permute-start | bytes 1425416 | tf_op jit(solution)/shard_map/ppermute | solution.py:102
  38.1 2.6 %collective-permute-start.7 = (bf16[128,3712]{1,0:T(8,128)(2,1)S(1)}, bf16[128,3712]{1,0:T(8,128)(2,1)S(1)}, u32[]{:S(2)}, u32[]{:S(2)}) collective-permute-start(bf16[128,3712]{1,0:T(8,128)(2,1)S(1)} %get-tuple-element.4), channel_id=1, source_target_pairs={{0,2},{2,0},{4,6},{6,4},{8,10},{10,8},{12,14},{14,12},{16,18},{18,... | collective-permute-start | bytes 2850824 | tf_op jit(solution)/shard_map/ppermute | solution.py:102
  39.1 2.2 %copy-start.6 = (bf16[1,3584,512]{2,1,0:T(8,128)(2,1)S(1)}, bf16[1,3584,512]{2,1,0:T(8,128)(2,1)}, u32[]{:S(2)}) copy-start(bf16[1,3584,512]{2,1,0:T(8,128)(2,1)} %param.12) | copy-start | bytes 11010052
  40.0 2.7 %collective-permute-start.14 = (bf16[128,3712]{1,0:T(8,128)(2,1)}, bf16[128,3712]{1,0:T(8,128)(2,1)S(1)}, u32[]{:S(2)}, u32[]{:S(2)}) collective-permute-start(bf16[128,3712]{1,0:T(8,128)(2,1)} %get-tuple-element.6), channel_id=1, source_target_pairs={{0,2},{2,0},{4,6},{6,4},{8,10},{10,8},{12,14},{14,12},{16,18},{18,... | collective-permute-start | bytes 2850824 | tf_op jit(solution)/shard_map/ppermute | solution.py:102
  44.1 9.2 %collective-permute-start.8 = (bf16[256,512]{1,0:T(8,128)(2,1)S(1)}, bf16[256,512]{1,0:T(8,128)(2,1)S(1)}, u32[]{:S(2)}, u32[]{:S(2)}) collective-permute-start(bf16[256,512]{1,0:T(8,128)(2,1)S(1)} %bitcast.105), channel_id=1, source_target_pairs={{0,1},{1,0},{2,3},{3,2},{4,5},{5,4},{6,7},{7,6},{8,9},{9,8},{10,11... | collective-permute-start | bytes 786440 | tf_op jit(solution)/shard_map/ppermute | solution.py:102
  45.4 12.8 %collective-permute-start.15 = (bf16[256,512]{1,0:T(8,128)(2,1)S(1)}, bf16[256,512]{1,0:T(8,128)(2,1)S(1)}, u32[]{:S(2)}, u32[]{:S(2)}) collective-permute-start(bf16[256,512]{1,0:T(8,128)(2,1)S(1)} %bitcast.104), channel_id=1, source_target_pairs={{0,1},{1,0},{2,3},{3,2},{4,5},{5,4},{6,7},{7,6},{8,9},{9,8},{10,11... | collective-permute-start | bytes 786440 | tf_op jit(solution)/shard_map/ppermute | solution.py:102
  46.6 6.7 %copy-start = (bf16[1,1024,1792]{2,1,0:T(8,128)(2,1)S(1)}, bf16[1,1024,1792]{2,1,0:T(8,128)(2,1)}, u32[]{:S(2)}) copy-start(bf16[1,1024,1792]{2,1,0:T(8,128)(2,1)} %param.13) | copy-start | bytes 11010052
  54.0 5.0 %collective-permute-start.9 = (bf16[128,1792]{1,0:T(8,128)(2,1)S(1)}, bf16[128,1792]{1,0:T(8,128)(2,1)S(1)}, u32[]{:S(2)}, u32[]{:S(2)}) collective-permute-start(bf16[128,1792]{1,0:T(8,128)(2,1)S(1)} %slice.251), channel_id=1, source_target_pairs={{0,2},{2,0},{4,6},{6,4},{8,10},{10,8},{12,14},{14,12},{16,18},{18,... | collective-permute-start | bytes 1376264 | tf_op jit(solution)/shard_map/ppermute | solution.py:102
  59.0 1.9 %collective-permute-start.16 = (bf16[128,1792]{1,0:T(8,128)(2,1)S(1)}, bf16[128,1792]{1,0:T(8,128)(2,1)S(1)}, u32[]{:S(2)}, u32[]{:S(2)}) collective-permute-start(bf16[128,1792]{1,0:T(8,128)(2,1)S(1)} %slice.250), channel_id=1, source_target_pairs={{0,2},{2,0},{4,6},{6,4},{8,10},{10,8},{12,14},{14,12},{16,18},{18,... | collective-permute-start | bytes 1376264 | tf_op jit(solution)/shard_map/ppermute | solution.py:102
  59.2 8.1 %collective-permute-start.10 = (bf16[64,1792]{1,0:T(8,128)(2,1)S(1)}, bf16[64,1792]{1,0:T(8,128)(2,1)S(1)}, u32[]{:S(2)}, u32[]{:S(2)}) collective-permute-start(bf16[64,1792]{1,0:T(8,128)(2,1)S(1)} %bitcast.107), channel_id=1, source_target_pairs={{0,4},{2,6},{4,0},{6,2},{8,12},{10,14},{12,8},{14,10},{16,20},{18,... | collective-permute-start | bytes 688136 | tf_op jit(solution)/shard_map/ppermute | solution.py:102
  61.0 7.8 %collective-permute-start.17 = (bf16[64,1792]{1,0:T(8,128)(2,1)S(1)}, bf16[64,1792]{1,0:T(8,128)(2,1)S(1)}, u32[]{:S(2)}, u32[]{:S(2)}) collective-permute-start(bf16[64,1792]{1,0:T(8,128)(2,1)S(1)} %bitcast.106), channel_id=1, source_target_pairs={{0,8},{2,10},{4,12},{6,14},{8,0},{10,2},{12,4},{14,6},{16,24},{18,... | collective-permute-start | bytes 688136 | tf_op jit(solution)/shard_map/ppermute | solution.py:102
  67.3 13.6 %copy-start.1 = (bf16[16,3584]{1,0:T(8,128)(2,1)S(1)}, bf16[16,3584]{1,0:T(8,128)(2,1)}, u32[]{:S(2)}) copy-start(bf16[16,3584]{1,0:T(8,128)(2,1)} %param.9) | copy-start | bytes 344068
  67.3 4.9 %collective-permute-start.11 = (bf16[32,1792]{1,0:T(8,128)(2,1)S(1)}, bf16[32,1792]{1,0:T(8,128)(2,1)S(1)}, u32[]{:S(2)}, u32[]{:S(2)}) collective-permute-start(bf16[32,1792]{1,0:T(8,128)(2,1)S(1)} %bitcast.110), channel_id=1, source_target_pairs={{0,8},{2,10},{4,12},{6,14},{8,0},{10,2},{12,4},{14,6},{16,24},{18,... | collective-permute-start | bytes 344072 | tf_op jit(solution)/shard_map/ppermute | solution.py:102
  68.9 17.0 %copy-start.5 = (s32[1,8]{1,0:T(1,128)S(1)}, s32[1,8]{1,0:T(1,128)}, u32[]{:S(2)}) copy-start(s32[1,8]{1,0:T(1,128)} %param.15) | copy-start | bytes 100
  68.9 6.8 %collective-permute-start.18 = (bf16[32,1792]{1,0:T(8,128)(2,1)S(1)}, bf16[32,1792]{1,0:T(8,128)(2,1)S(1)}, u32[]{:S(2)}, u32[]{:S(2)}) collective-permute-start(bf16[32,1792]{1,0:T(8,128)(2,1)S(1)} %bitcast.111), channel_id=1, source_target_pairs={{0,4},{2,6},{4,0},{6,2},{8,12},{10,14},{12,8},{14,10},{16,20},{18,... | collective-permute-start | bytes 344072 | tf_op jit(solution)/shard_map/ppermute | solution.py:102
  72.2 14.1 %copy-start.3 = (f32[3584]{0:T(1024)S(1)}, f32[3584]{0:T(1024)}, u32[]{:S(2)}) copy-start(f32[3584]{0:T(1024)} %param.17) | copy-start | bytes 43012
  72.2 5.9 %collective-permute-start.12 = (bf16[16,1792]{1,0:T(8,128)(2,1)S(1)}, bf16[16,1792]{1,0:T(8,128)(2,1)S(1)}, u32[]{:S(2)}, u32[]{:S(2)}) collective-permute-start(bf16[16,1792]{1,0:T(8,128)(2,1)S(1)} %fusion.50), channel_id=1, source_target_pairs={{0,16},{2,18},{4,20},{6,22},{8,24},{10,26},{12,28},{14,30},{16,0},... | collective-permute-start | bytes 172040 | tf_op jit(solution)/shard_map/ppermute | solution.py:102
  75.7 5.1 %collective-permute-start.19 = (bf16[16,1792]{1,0:T(8,128)(2,1)S(1)}, bf16[16,1792]{1,0:T(8,128)(2,1)S(1)}, u32[]{:S(2)}, u32[]{:S(2)}) collective-permute-start(bf16[16,1792]{1,0:T(8,128)(2,1)S(1)} %fusion.51), channel_id=1, source_target_pairs={{0,16},{2,18},{4,20},{6,22},{8,24},{10,26},{12,28},{14,30},{16,0},... | collective-permute-start | bytes 172040 | tf_op jit(solution)/shard_map/ppermute | solution.py:102
  80.9 4.9 %collective-permute-start.20 = (bf16[32,1792]{1,0:T(8,128)(2,1)S(1)}, bf16[32,1792]{1,0:T(8,128)(2,1)S(1)}, u32[]{:S(2)}, u32[]{:S(2)}) collective-permute-start(bf16[32,1792]{1,0:T(8,128)(2,1)S(1)} %bitcast.103), channel_id=1, source_target_pairs={{0,1},{1,0},{2,3},{3,2},{4,5},{5,4},{6,7},{7,6},{8,9},{9,8},{10,11... | collective-permute-start | bytes 344072 | tf_op jit(solution)/shard_map/ppermute | solution.py:102
  85.9 1.1 %copy-start.2 = (bf16[16,3584]{1,0:T(8,128)(2,1)}, bf16[16,3584]{1,0:T(8,128)(2,1)S(1)}, u32[]{:S(2)}) copy-start(bf16[16,3584]{1,0:T(8,128)(2,1)S(1)} %slice_bitcast_fusion.3) | copy-start | bytes 344068

commit v2 on v1

--- a/solution.py
+++ b/solution.py
@@ -97,9 +97,15 @@
     return (rows * scale * gain[None, :]).astype(jnp.bfloat16)[None]
 
 
-def swap(array, axis, bit):
-    size = lax.axis_size(axis)
-    return lax.ppermute(array, axis, [(i, i ^ bit) for i in range(size)])
+X, CORE, Y, NEAR, FAR = 1, 2, 4, 8, 16
+
+
+def swap(array, name, bit, bit_on_second_core=None):
+    bits = (bit, bit if bit_on_second_core is None else bit_on_second_core)
+    size = lax.axis_size("expert") * lax.axis_size("req")
+    pairs = [(i, i ^ bits[1 if i & CORE else 0]) for i in range(size)]
+    with jax.named_scope(name):
+        return lax.ppermute(array, ("expert", "req"), pairs)
 
 
 def three_parts(value):
@@ -110,14 +116,8 @@
     return [first, second, third]
 
 
-CORE, Y, NEAR, FAR = ("expert", 1), ("expert", 2), ("expert", 4), ("expert", 8)
-X = ("req", 1)
-
-
-def gather(block, steps):
-    for axis, bit in steps:
-        block = jnp.concatenate([block, swap(block, axis, bit)], axis=0)
-    return block
+def blocks_of(array, order, length):
+    return jnp.concatenate([array[i * length : (i + 1) * length] for i in order], axis=0)
 
 
 def gathered_plan(
@@ -135,13 +135,12 @@
     tree_len, features = tree_hidden.shape
     accept_len = accept_pos.shape[1]
     me = lax.axis_index("expert")
+    first_core = me % 2 == 0
     side = lax.axis_index("req")
     hidden_half = w_up.shape[2]
     feature_half = w_down.shape[2]
+
     half = tree_len // 2
-
-    w_own = lax.dynamic_slice_in_dim(w_down[0], side * hidden_half, hidden_half, 0)
-    w_other = lax.dynamic_slice_in_dim(w_down[0], (1 - side) * hidden_half, hidden_half, 0)
 
     experts = jnp.arange(expert_count, dtype=jnp.int32)
     dense = jnp.sum(
@@ -151,70 +150,111 @@
     selector = selector_of(accept_pos, accept_count, tree_len)
     selector = jnp.pad(selector, ((0, tree_len - accept_len), (0, 0)))
     extra = jnp.concatenate(three_parts(dense) + [selector], axis=1)
+    width = extra.shape[1]
+    extra = jnp.concatenate([extra[:half], extra[half:]], axis=1)
     extra = jnp.pad(extra, ((0, 0), (0, -extra.shape[1] % 128)))
-    rows = jnp.concatenate([tree_hidden, extra], axis=1)
-
-    steps = [(FAR, NEAR, Y, X, CORE), (FAR, NEAR, X, Y, CORE)]
-    blocks = [gather(rows[k * half : (k + 1) * half], steps[k]) for k in range(2)]
+
+    there = swap(tree_hidden, "rows", FAR, NEAR)
+    extra_there = swap(extra, "extra", FAR, NEAR)
+    blocks = [
+        jnp.concatenate([tree_hidden[:half], there[:half]], axis=0),
+        jnp.concatenate(
+            [
+                jnp.concatenate([tree_hidden[half:], there[half:]], axis=0),
+                jnp.concatenate([extra, extra_there], axis=0),
+            ],
+            axis=1,
+        ),
+    ]
+    for step, bits in ((1, (NEAR, FAR)), (2, (Y, X)), (3, (X, Y))):
+        blocks = [
+            jnp.concatenate([blocks[k], swap(blocks[k], f"rows_{k}_{step}", *bits)], axis=0)
+            for k in range(2)
+        ]
+    own = blocks
+    other = [swap(own[k], f"rows_{k}_core", CORE) for k in range(2)]
 
     here = (experts == me).astype(jnp.float32)
-    own, weight = [], []
+
+    def up(part):
+        return jax.nn.silu(
+            jnp.dot(part[:, :features], w_up[0], preferred_element_type=jnp.float32)
+        ).astype(jnp.bfloat16)
+
+    def weights(block, chunk):
+        at = features + chunk * width
+        parts = block[:, at : at + 3 * expert_count].astype(jnp.float32)
+        total = sum(parts[:, j * expert_count : (j + 1) * expert_count] for j in range(3))
+        return jnp.sum(total * here[None, :], axis=1, keepdims=True)
+
+    w_late = lax.optimization_barrier((w_down[0], own[0][:1, :128]))[0]
+    w_own = lax.dynamic_slice_in_dim(w_late, side * hidden_half, hidden_half, 0)
+    w_other = lax.dynamic_slice_in_dim(w_late, (1 - side) * hidden_half, hidden_half, 0)
+
+    span = own[0].shape[0]
+    last = lambda part: blocks_of(part, (1, 0), span // 2)
+    last_but_one = lambda part: blocks_of(part, (1, 0, 3, 2), span // 4)
+
+    order_first = [x * 8 + near * 2 + far for x in (0, 1) for near in (0, 1) for far in (0, 1)]
+    order_second = [y * 8 + x * 4 + far * 2 for x in (0, 1) for y in (0, 1) for far in (0, 1)]
+
+    acts, acts_there = [], []
     for k in range(2):
-        own.append(
-            jax.nn.silu(
-                jnp.dot(blocks[k][:, :features], w_up[0], preferred_element_type=jnp.float32)
-            ).astype(jnp.bfloat16)
+        acts.append((up(own[k]), up(other[k])))
+        turned = (
+            jnp.where(first_core, last(acts[k][0]), last_but_one(acts[k][0])),
+            jnp.where(first_core, last_but_one(acts[k][1]), last(acts[k][1])),
         )
-        parts = blocks[k][:, features:].astype(jnp.float32)
-        total = sum(parts[:, j * expert_count : (j + 1) * expert_count] for j in range(3))
-        weight.append(jnp.sum(total * here[None, :], axis=1, keepdims=True))
-    other = []
-    for k in range(2):
-        below = 1 << steps[k].index(X)
-        turned = own[k].reshape(-1, 2, below * half, hidden_half)[:, ::-1]
-        other.append(swap(turned.reshape(own[k].shape), *X))
+        acts_there.append(swap(jnp.concatenate(turned, axis=0), f"acts_{k}", X))
+
     sums = []
     for k in range(2):
-        produced = jnp.dot(own[k], w_own, preferred_element_type=jnp.float32) + jnp.dot(
-            other[k], w_other, preferred_element_type=jnp.float32
+
+        def down(acts_here, acts_there, block):
+            produced = jnp.dot(acts_here, w_own, preferred_element_type=jnp.float32) + jnp.dot(
+                acts_there, w_other, preferred_element_type=jnp.float32
+            )
+            return produced.astype(jnp.bfloat16).astype(jnp.float32) * weights(block, k)
+
+        away = down(acts[k][1], acts_there[k][span:], other[1]).astype(jnp.bfloat16)
+        total = down(acts[k][0], acts_there[k][:span], own[1])
+        total = total + swap(away, f"sums_{k}_core", CORE).astype(jnp.float32)
+        away = jnp.where(
+            first_core,
+            blocks_of(total, [i + 4 for i in order_first], half),
+            blocks_of(total, [i + 1 for i in order_second], half),
+        ).astype(jnp.bfloat16)
+        total = jnp.where(
+            first_core, blocks_of(total, order_first, half), blocks_of(total, order_second, half)
         )
-        sums.append(produced.astype(jnp.bfloat16).astype(jnp.float32) * weight[k])
-
-    back = [(CORE, Y, NEAR, FAR), (CORE, NEAR, Y, FAR)]
-    done = []
-    for k in range(2):
-        names = list(reversed(steps[k]))
-        total = sums[k].reshape((2,) * len(names) + (half, feature_half))
-        for step in back[k]:
-            at = names.index(step)
-            keep = lax.index_in_dim(total, 0, at, keepdims=False)
-            send = lax.index_in_dim(total, 1, at, keepdims=False).astype(jnp.bfloat16)
-            shape = keep.shape
-            received = swap(send.reshape(-1, feature_half), *step).reshape(shape)
-            total = keep + received.astype(jnp.float32)
-            names.remove(step)
-        done.append(total)
-    mixed = jnp.concatenate(done, axis=1)
-
-    place = [len(set(steps[k][: steps[k].index(X)])) for k in range(2)]
-    second = jnp.concatenate(
-        [blocks[k][half << place[k] : (half << place[k]) + half] for k in range(2)], axis=0
-    )
-    pair_hidden = jnp.stack([tree_hidden, second[:, :features]])
-    pair_part = lax.dynamic_slice_in_dim(pair_hidden, side * feature_half, feature_half, 2)
-    layer_part = (pair_part.astype(jnp.float32) + mixed).astype(jnp.bfloat16)
-    received = swap(layer_part.reshape(2 * tree_len, feature_half), *X)
-    received = received.reshape(2, tree_len, feature_half)[::-1]
+        total = total + swap(away, f"sums_{k}_0", Y, NEAR).astype(jnp.float32)
+        for step, bits in ((1, (NEAR, Y)), (2, (FAR, FAR))):
+            shaped = total.reshape(2, 2, -1, feature_half)
+            away = shaped[:, 1].reshape(-1, feature_half).astype(jnp.bfloat16)
+            received = swap(away, f"sums_{k}_{step}", *bits)
+            total = shaped[:, 0].reshape(-1, feature_half) + received.astype(jnp.float32)
+        sums.append(total.reshape(2, half, feature_half))
+    total = jnp.concatenate(sums, axis=1).reshape(2 * tree_len, feature_half)
+
+    second = [
+        jnp.where(first_core, block[8 * half : 9 * half], block[4 * half : 5 * half])
+        for block in own
+    ]
+    pair_hidden = jnp.concatenate([tree_hidden, second[0], second[1][:, :features]], axis=0)
+    pair_part = lax.dynamic_slice_in_dim(pair_hidden, side * feature_half, feature_half, 1)
+    layer_part = (pair_part.astype(jnp.float32) + total).astype(jnp.bfloat16)
+    received = blocks_of(swap(layer_part, "layer", X), (1, 0), tree_len)
     layer_pair = jnp.where(
         side == 0,
-        jnp.concatenate([layer_part, received], axis=2),
-        jnp.concatenate([received, layer_part], axis=2),
-    )
-    layer_local = layer_pair[0]
+        jnp.concatenate([layer_part, received], axis=1),
+        jnp.concatenate([received, layer_part], axis=1),
+    )
+    layer_local = layer_pair[:tree_len]
+    stays = draft_owner[0] == side
+    chosen = jnp.where(stays, layer_local, layer_pair[tree_len:])
     at = features + 3 * expert_count
-    stays = draft_owner[0] == side
-    chosen = jnp.where(stays, layer_local, layer_pair[1])
-    chosen_selector = jnp.where(stays, rows[:accept_len, at : at + tree_len], second[:accept_len, at : at + tree_len])
+    there = jnp.concatenate([second[1][:, at : at + tree_len], second[1][:, at + width : at + width + tree_len]], axis=0)
+    chosen_selector = jnp.where(stays, selector, there)[:accept_len]
     incoming = jnp.dot(chosen_selector, chosen, preferred_element_type=jnp.float32)
     return (layer_local, norm_rows(incoming, mtp_gain))
 

time: 87.2 us -> 81.9 us (0.939)
  waiting for transfers between devices: 37.2 us -> 32.5 us
  local copies, waits for them, and re-layouts: 7.58 us -> 4.26 us
  starting transfers between devices: 29.5 us -> 32.4 us
    ppermute x21, waiting for transfers between devices: 37.2 us -> 32.5 us  [swap(): return lax.ppermute(array, ('expert', 'req'), pairs)]
    unnamed x23 -> x46, local copies, waits for them, and re-layouts: 6.13 us -> 2.94 us
    ppermute x21, starting transfers between devices: 29.5 us -> 32.4 us  [swap(): return lax.ppermute(array, ('expert', 'req'), pairs)]
    concatenate x4 -> x5, local copies, waits for them, and re-layouts: 1.18 us -> 0.06 us  [the longest x1 0.03 us: gathered_plan(): jnp.concatenate([blocks[k], swap(blocks[k], f'rows_{k}_{step}', *bits)],...]
    slice x10 -> x24, local copies, waits for them, and re-layouts: 0.21 us -> 1.25 us  [the longest x1 0.86 us: gathered_plan(): tree_hidden[:half]]
    dot_general x6 -> x12, matrix products: 6.65 us -> 6.15 us  [the longest x4 2.77 us: up(): jnp.dot(part[:, :features], w_up[0], preferred_element_type=jnp.float32)]
  transfers between devices with their start and end apart: 21 -> 21, of which waited for: 17 -> 14; matrix products, arithmetic and copies ran while one was open for 13% -> 14% of each run, Pallas kernels for 0% -> 0%
where the time goes in v2:
time: 81.9 us; the launch traced here: 81.6 us
  waiting for transfers between devices  32.5 us (40%)
  starting transfers between devices  32.4 us (40%)
  matrix products  6.42 us (8%)
  local copies, waits for them, and re-layouts  4.26 us (5%)
  other arithmetic  3.23 us (4%)
  between operations  2.79 us (3%)
    ppermute x21, waiting for transfers between devices, swap(): return lax.ppermute(array, ('expert', 'req'), pairs)  32.5 us
    ppermute x21, starting transfers between devices, swap(): return lax.ppermute(array, ('expert', 'req'), pairs)  32.4 us
    unnamed x46, local copies, waits for them, and re-layouts  2.94 us
    dot_general x4, matrix products, up(): jnp.dot(part[:, :features], w_up[0], preferred_element_type=jnp.float32)  2.77 us
    dot_general x4, matrix products, down(): jnp.dot(acts_there, w_other, preferred_element_type=jnp.float32)  1.72 us
    dot_general x4, matrix products, down(): jnp.dot(acts_here, w_own, preferred_element_type=jnp.float32)  1.67 us
  transfers between devices with their start and end apart: 21, of which 14 were waited for; matrix products, arithmetic and copies ran while one was open for 14% of the time, Pallas kernels for 0%

profile of v2, /device:TPU:0, one launch (start us, length us, event | category | flops | bytes accessed | tf_op | source)
XLA Modules:
  0.0 81.6 jit_solution(219012134622573985)
XLA Ops:
  0.6 4.1 %collective-permute-start = (bf16[16,3584]{1,0:T(8,128)(2,1)}, bf16[16,3584]{1,0:T(8,128)(2,1)S(1)}, u32[]{:S(2)}, u32[]{:S(2)}) collective-permute-start(bf16[16,3584]{1,0:T(8,128)(2,1)} %param.9), channel_id=1, source_target_pairs={{0,16},{1,17},{2,10},{3,11},{4,20},{5,21},{6,14},{7,15},{8,24},{9,... | collective-permute-start | bytes 344072 | tf_op jit(solution)/shard_map/rows/ppermute | solution.py:108
  4.7 0.8 copy.13
  8.0 0.9 %fusion.104 = (bf16[8,3584]{1,0:T(8,128)(2,1)S(1)}, bf16[128,3584]{1,0:T(8,128)(2,1)S(1)}, bf16[8,3584]{1,0:T(8,128)(2,1)S(1)}) fusion(bf16[16,3584]{1,0:T(8,128)(2,1)} %param.9), kind=kLoop, calls=%fused_computation.198 | loop fusion | bytes 286720 | tf_op jit(solution)/shard_map/slice | solution.py:160
  9.6 2.0 %collective-permute-start.1 = (bf16[16,3584]{1,0:T(8,128)(2,1)S(1)}, bf16[16,3584]{1,0:T(8,128)(2,1)S(1)}, u32[]{:S(2)}, u32[]{:S(2)}) collective-permute-start(bf16[16,3584]{1,0:T(8,128)(2,1)S(1)} %pad_maximum_fusion.8), channel_id=1, source_target_pairs={{0,8},{1,9},{2,18},{3,19},{4,12},{5,13},{6,22},{7,23},{8,0},{9,1},... | collective-permute-start | bytes 344072 | tf_op jit(solution)/shard_map/rows_0_1/ppermute | solution.py:108
  11.5 0.9 %collective-permute-done.4 = bf16[8,128]{1,0:T(8,128)(2,1)S(1)} collective-permute-done((bf16[8,128]{1,0:T(8,128)(2,1)S(1)}, bf16[8,128]{1,0:T(8,128)(2,1)S(1)}, u32[]{:S(2)}, u32[]{:S(2)}) %collective-permute-start.4) | collective-permute-done | bytes 2080 | tf_op jit(solution)/shard_map/extra/ppermute | solution.py:108
  12.5 1.7 %collective-permute-start.5 = (bf16[16,3712]{1,0:T(8,128)(2,1)S(1)}, bf16[16,3712]{1,0:T(8,128)(2,1)S(1)}, u32[]{:S(2)}, u32[]{:S(2)}) collective-permute-start(bf16[16,3712]{1,0:T(8,128)(2,1)S(1)} %maximum_maximum_fusion), channel_id=1, source_target_pairs={{0,8},{1,9},{2,18},{3,19},{4,12},{5,13},{6,22},{7,23},{8,0},{9,1},... | collective-permute-start | bytes 356360 | tf_op jit(solution)/shard_map/rows_1_1/ppermute | solution.py:108
  14.2 1.3 %collective-permute-done.1 = bf16[16,3584]{1,0:T(8,128)(2,1)S(1)} collective-permute-done((bf16[16,3584]{1,0:T(8,128)(2,1)S(1)}, bf16[16,3584]{1,0:T(8,128)(2,1)S(1)}, u32[]{:S(2)}, u32[]{:S(2)}) %collective-permute-start.1) | collective-permute-done | bytes 114720 | tf_op jit(solution)/shard_map/rows_0_1/ppermute | solution.py:108
  15.5 2.0 %collective-permute-start.2 = (bf16[32,3584]{1,0:T(8,128)(2,1)S(1)}, bf16[32,3584]{1,0:T(8,128)(2,1)S(1)}, u32[]{:S(2)}, u32[]{:S(2)}) collective-permute-start(bf16[32,3584]{1,0:T(8,128)(2,1)S(1)} %pad_maximum_fusion.6), channel_id=1, source_target_pairs={{0,4},{1,5},{2,3},{3,2},{4,0},{5,1},{6,7},{7,6},{8,12},{9,13},{10,... | collective-permute-start | bytes 688136 | tf_op jit(solution)/shard_map/rows_0_2/ppermute | solution.py:108
  17.6 1.5 %collective-permute-start.6 = (bf16[32,3712]{1,0:T(8,128)(2,1)S(1)}, bf16[32,3712]{1,0:T(8,128)(2,1)S(1)}, u32[]{:S(2)}, u32[]{:S(2)}) collective-permute-start(bf16[32,3712]{1,0:T(8,128)(2,1)S(1)} %pad_maximum_fusion.5), channel_id=1, source_target_pairs={{0,4},{1,5},{2,3},{3,2},{4,0},{5,1},{6,7},{7,6},{8,12},{9,13},{10,... | collective-permute-start | bytes 712712 | tf_op jit(solution)/shard_map/rows_1_2/ppermute | solution.py:108
  19.1 2.5 %collective-permute-done.2 = bf16[32,3584]{1,0:T(8,128)(2,1)S(1)} collective-permute-done((bf16[32,3584]{1,0:T(8,128)(2,1)S(1)}, bf16[32,3584]{1,0:T(8,128)(2,1)S(1)}, u32[]{:S(2)}, u32[]{:S(2)}) %collective-permute-start.2) | collective-permute-done | bytes 229408 | tf_op jit(solution)/shard_map/rows_0_2/ppermute | solution.py:108
  21.6 2.1 %collective-permute-start.3 = (bf16[64,3584]{1,0:T(8,128)(2,1)S(1)}, bf16[64,3584]{1,0:T(8,128)(2,1)S(1)}, u32[]{:S(2)}, u32[]{:S(2)}) collective-permute-start(bf16[64,3584]{1,0:T(8,128)(2,1)S(1)} %pad_maximum_fusion.2), channel_id=1, source_target_pairs={{0,1},{1,0},{2,6},{3,7},{4,5},{5,4},{6,2},{7,3},{8,9},{9,8},{10,14... | collective-permute-start | bytes 1376264 | tf_op jit(solution)/shard_map/rows_0_3/ppermute | solution.py:108
  23.7 2.5 %collective-permute-done.6 = bf16[32,3712]{1,0:T(8,128)(2,1)S(1)} collective-permute-done((bf16[32,3712]{1,0:T(8,128)(2,1)S(1)}, bf16[32,3712]{1,0:T(8,128)(2,1)S(1)}, u32[]{:S(2)}, u32[]{:S(2)}) %collective-permute-start.6) | collective-permute-done | bytes 237600 | tf_op jit(solution)/shard_map/rows_1_2/ppermute | solution.py:108
  26.3 2.5 %collective-permute-start.7 = (bf16[64,3712]{1,0:T(8,128)(2,1)S(1)}, bf16[64,3712]{1,0:T(8,128)(2,1)S(1)}, u32[]{:S(2)}, u32[]{:S(2)}) collective-permute-start(bf16[64,3712]{1,0:T(8,128)(2,1)S(1)} %pad_maximum_fusion.1), channel_id=1, source_target_pairs={{0,1},{1,0},{2,6},{3,7},{4,5},{5,4},{6,2},{7,3},{8,9},{9,8},{10,14... | collective-permute-start | bytes 1425416 | tf_op jit(solution)/shard_map/rows_1_3/ppermute | solution.py:108
  28.8 1.4 %collective-permute-done.3 = bf16[64,3584]{1,0:T(8,128)(2,1)S(1)} collective-permute-done((bf16[64,3584]{1,0:T(8,128)(2,1)S(1)}, bf16[64,3584]{1,0:T(8,128)(2,1)S(1)}, u32[]{:S(2)}, u32[]{:S(2)}) %collective-permute-start.3) | collective-permute-done | bytes 458784 | tf_op jit(solution)/shard_map/rows_0_3/ppermute | solution.py:108
  31.1 1.2 %copy-done = bf16[1,1024,1792]{2,1,0:T(8,128)(2,1)S(1)} copy-done((bf16[1,1024,1792]{2,1,0:T(8,128)(2,1)S(1)}, bf16[1,1024,1792]{2,1,0:T(8,128)(2,1)}, u32[]{:S(2)}) %copy-start) | copy-done | bytes 3670040
  32.7 2.8 %collective-permute-done.7 = bf16[64,3712]{1,0:T(8,128)(2,1)S(1)} collective-permute-done((bf16[64,3712]{1,0:T(8,128)(2,1)S(1)}, bf16[64,3712]{1,0:T(8,128)(2,1)S(1)}, u32[]{:S(2)}, u32[]{:S(2)}) %collective-permute-start.7) | collective-permute-done | bytes 475168 | tf_op jit(solution)/shard_map/rows_1_3/ppermute | solution.py:108
  37.7 2.1 %collective-permute-start.9 = (bf16[256,512]{1,0:T(8,128)(2,1)S(1)}, bf16[256,512]{1,0:T(8,128)(2,1)S(1)}, u32[]{:S(2)}, u32[]{:S(2)}) collective-permute-start(bf16[256,512]{1,0:T(8,128)(2,1)S(1)} %pad_maximum_fusion.3), channel_id=1, source_target_pairs={{0,1},{1,0},{2,3},{3,2},{4,5},{5,4},{6,7},{7,6},{8,9},{9,8},{10,11... | collective-permute-start | bytes 786440 | tf_op jit(solution)/shard_map/acts_0/ppermute | solution.py:108
  41.6 5.4 %collective-permute-done.9 = bf16[256,512]{1,0:T(8,128)(2,1)S(1)} collective-permute-done((bf16[256,512]{1,0:T(8,128)(2,1)S(1)}, bf16[256,512]{1,0:T(8,128)(2,1)S(1)}, u32[]{:S(2)}, u32[]{:S(2)}) %collective-permute-start.9) | collective-permute-done | bytes 262176 | tf_op jit(solution)/shard_map/acts_0/ppermute | solution.py:108
  47.9 4.5 %collective-permute-done.15 = bf16[256,512]{1,0:T(8,128)(2,1)S(1)} collective-permute-done((bf16[256,512]{1,0:T(8,128)(2,1)S(1)}, bf16[256,512]{1,0:T(8,128)(2,1)S(1)}, u32[]{:S(2)}, u32[]{:S(2)}) %collective-permute-start.15) | collective-permute-done | bytes 262176 | tf_op jit(solution)/shard_map/acts_1/ppermute | solution.py:108
  53.7 1.8 %collective-permute-start.12 = (bf16[64,1792]{1,0:T(8,128)(2,1)S(1)}, bf16[64,1792]{1,0:T(8,128)(2,1)S(1)}, u32[]{:S(2)}, u32[]{:S(2)}) collective-permute-start(bf16[64,1792]{1,0:T(8,128)(2,1)S(1)} %fusion.39), channel_id=1, source_target_pairs={{0,4},{1,5},{2,10},{3,11},{4,0},{5,1},{6,14},{7,15},{8,12},{9,13},... | collective-permute-start | bytes 688136 | tf_op jit(solution)/shard_map/sums_0_0/ppermute | solution.py:108
  56.3 1.0 %collective-permute-start.17 = (bf16[64,1792]{1,0:T(8,128)(2,1)S(1)}, bf16[64,1792]{1,0:T(8,128)(2,1)S(1)}, u32[]{:S(2)}, u32[]{:S(2)}) collective-permute-start(bf16[64,1792]{1,0:T(8,128)(2,1)S(1)} %fusion.41), channel_id=1, source_target_pairs={{0,4},{1,5},{2,10},{3,11},{4,0},{5,1},{6,14},{7,15},{8,12},{9,13},... | collective-permute-start | bytes 688136 | tf_op jit(solution)/shard_map/sums_1_0/ppermute | solution.py:108
  57.4 2.4 %collective-permute-done.12 = bf16[64,1792]{1,0:T(8,128)(2,1)S(1)} collective-permute-done((bf16[64,1792]{1,0:T(8,128)(2,1)S(1)}, bf16[64,1792]{1,0:T(8,128)(2,1)S(1)}, u32[]{:S(2)}, u32[]{:S(2)}) %collective-permute-start.12) | collective-permute-done | bytes 229408 | tf_op jit(solution)/shard_map/sums_0_0/ppermute | solution.py:108
  59.9 1.4 %collective-permute-start.13 = (bf16[32,1792]{1,0:T(8,128)(2,1)S(1)}, bf16[32,1792]{1,0:T(8,128)(2,1)S(1)}, u32[]{:S(2)}, u32[]{:S(2)}) collective-permute-start(bf16[32,1792]{1,0:T(8,128)(2,1)S(1)} %bitcast.81), channel_id=1, source_target_pairs={{0,8},{1,9},{2,6},{3,7},{4,12},{5,13},{6,2},{7,3},{8,0},{9,1},{10,... | collective-permute-start | bytes 344072 | tf_op jit(solution)/shard_map/sums_0_1/ppermute | solution.py:108
  61.2 1.3 %collective-permute-done.17 = bf16[64,1792]{1,0:T(8,128)(2,1)S(1)} collective-permute-done((bf16[64,1792]{1,0:T(8,128)(2,1)S(1)}, bf16[64,1792]{1,0:T(8,128)(2,1)S(1)}, u32[]{:S(2)}, u32[]{:S(2)}) %collective-permute-start.17) | collective-permute-done | bytes 229408 | tf_op jit(solution)/shard_map/sums_1_0/ppermute | solution.py:108
  62.7 1.0 %collective-permute-start.18 = (bf16[32,1792]{1,0:T(8,128)(2,1)S(1)}, bf16[32,1792]{1,0:T(8,128)(2,1)S(1)}, u32[]{:S(2)}, u32[]{:S(2)}) collective-permute-start(bf16[32,1792]{1,0:T(8,128)(2,1)S(1)} %bitcast.82), channel_id=1, source_target_pairs={{0,8},{1,9},{2,6},{3,7},{4,12},{5,13},{6,2},{7,3},{8,0},{9,1},{10,... | collective-permute-start | bytes 344072 | tf_op jit(solution)/shard_map/sums_1_1/ppermute | solution.py:108
  63.7 1.0 %collective-permute-done.13 = bf16[32,1792]{1,0:T(8,128)(2,1)S(1)} collective-permute-done((bf16[32,1792]{1,0:T(8,128)(2,1)S(1)}, bf16[32,1792]{1,0:T(8,128)(2,1)S(1)}, u32[]{:S(2)}, u32[]{:S(2)}) %collective-permute-start.13) | collective-permute-done | bytes 114720 | tf_op jit(solution)/shard_map/sums_0_1/ppermute | solution.py:108
  64.8 5.0 %collective-permute-start.14 = (bf16[16,1792]{1,0:T(8,128)(2,1)S(1)}, bf16[16,1792]{1,0:T(8,128)(2,1)S(1)}, u32[]{:S(2)}, u32[]{:S(2)}) collective-permute-start(bf16[16,1792]{1,0:T(8,128)(2,1)S(1)} %fusion.76), channel_id=1, source_target_pairs={{0,16},{1,17},{2,18},{3,19},{4,20},{5,21},{6,22},{7,23},{8,24},{9,... | collective-permute-start | bytes 172040 | tf_op jit(solution)/shard_map/sums_0_2/ppermute | solution.py:108
  69.8 2.4 %collective-permute-start.19 = (bf16[16,1792]{1,0:T(8,128)(2,1)S(1)}, bf16[16,1792]{1,0:T(8,128)(2,1)S(1)}, u32[]{:S(2)}, u32[]{:S(2)}) collective-permute-start(bf16[16,1792]{1,0:T(8,128)(2,1)S(1)} %fusion.77), channel_id=1, source_target_pairs={{0,16},{1,17},{2,18},{3,19},{4,20},{5,21},{6,22},{7,23},{8,24},{9,... | collective-permute-start | bytes 172040 | tf_op jit(solution)/shard_map/sums_1_2/ppermute | solution.py:108
  72.2 1.2 %collective-permute-done.14 = bf16[16,1792]{1,0:T(8,128)(2,1)S(1)} collective-permute-done((bf16[16,1792]{1,0:T(8,128)(2,1)S(1)}, bf16[16,1792]{1,0:T(8,128)(2,1)S(1)}, u32[]{:S(2)}, u32[]{:S(2)}) %collective-permute-start.14) | collective-permute-done | bytes 57376 | tf_op jit(solution)/shard_map/sums_0_2/ppermute | solution.py:108
  73.5 2.1 %collective-permute-done.19 = bf16[16,1792]{1,0:T(8,128)(2,1)S(1)} collective-permute-done((bf16[16,1792]{1,0:T(8,128)(2,1)S(1)}, bf16[16,1792]{1,0:T(8,128)(2,1)S(1)}, u32[]{:S(2)}, u32[]{:S(2)}) %collective-permute-start.19) | collective-permute-done | bytes 57376 | tf_op jit(solution)/shard_map/sums_1_2/ppermute | solution.py:108
  75.7 1.6 %collective-permute-start.20 = (bf16[32,1792]{1,0:T(8,128)(2,1)S(1)}, bf16[32,1792]{1,0:T(8,128)(2,1)S(1)}, u32[]{:S(2)}, u32[]{:S(2)}) collective-permute-start(bf16[32,1792]{1,0:T(8,128)(2,1)S(1)} %fusion.54), channel_id=1, source_target_pairs={{0,1},{1,0},{2,3},{3,2},{4,5},{5,4},{6,7},{7,6},{8,9},{9,8},{10,11... | collective-permute-start | bytes 344072 | tf_op jit(solution)/shard_map/layer/ppermute | solution.py:108
  77.3 3.2 %collective-permute-done.20 = bf16[32,1792]{1,0:T(8,128)(2,1)S(1)} collective-permute-done((bf16[32,1792]{1,0:T(8,128)(2,1)S(1)}, bf16[32,1792]{1,0:T(8,128)(2,1)S(1)}, u32[]{:S(2)}, u32[]{:S(2)}) %collective-permute-start.20) | collective-permute-done | bytes 114720 | tf_op jit(solution)/shard_map/layer/ppermute | solution.py:108
  (137 shorter events, 11.5 us)
Async XLA Ops:
  0.6 8.9 %collective-permute-start = (bf16[16,3584]{1,0:T(8,128)(2,1)}, bf16[16,3584]{1,0:T(8,128)(2,1)S(1)}, u32[]{:S(2)}, u32[]{:S(2)}) collective-permute-start(bf16[16,3584]{1,0:T(8,128)(2,1)} %param.9), channel_id=1, source_target_pairs={{0,16},{1,17},{2,10},{3,11},{4,20},{5,21},{6,14},{7,15},{8,24},{9,... | collective-permute-start | bytes 344072 | tf_op jit(solution)/shard_map/rows/ppermute | solution.py:108
  7.9 4.5 %collective-permute-start.4 = (bf16[8,128]{1,0:T(8,128)(2,1)S(1)}, bf16[8,128]{1,0:T(8,128)(2,1)S(1)}, u32[]{:S(2)}, u32[]{:S(2)}) collective-permute-start(bf16[8,128]{1,0:T(8,128)(2,1)S(1)} %pad_maximum_fusion.12), channel_id=1, source_target_pairs={{0,16},{1,17},{2,10},{3,11},{4,20},{5,21},{6,14},{7,15},{8,24},{9,... | collective-permute-start | bytes 6152 | tf_op jit(solution)/shard_map/extra/ppermute | solution.py:108
  9.6 6.0 %collective-permute-start.1 = (bf16[16,3584]{1,0:T(8,128)(2,1)S(1)}, bf16[16,3584]{1,0:T(8,128)(2,1)S(1)}, u32[]{:S(2)}, u32[]{:S(2)}) collective-permute-start(bf16[16,3584]{1,0:T(8,128)(2,1)S(1)} %pad_maximum_fusion.8), channel_id=1, source_target_pairs={{0,8},{1,9},{2,18},{3,19},{4,12},{5,13},{6,22},{7,23},{8,0},{9,1},... | collective-permute-start | bytes 344072 | tf_op jit(solution)/shard_map/rows_0_1/ppermute | solution.py:108
  12.5 5.0 %collective-permute-start.5 = (bf16[16,3712]{1,0:T(8,128)(2,1)S(1)}, bf16[16,3712]{1,0:T(8,128)(2,1)S(1)}, u32[]{:S(2)}, u32[]{:S(2)}) collective-permute-start(bf16[16,3712]{1,0:T(8,128)(2,1)S(1)} %maximum_maximum_fusion), channel_id=1, source_target_pairs={{0,8},{1,9},{2,18},{3,19},{4,12},{5,13},{6,22},{7,23},{8,0},{9,1},... | collective-permute-start | bytes 356360 | tf_op jit(solution)/shard_map/rows_1_1/ppermute | solution.py:108
  15.5 6.1 %collective-permute-start.2 = (bf16[32,3584]{1,0:T(8,128)(2,1)S(1)}, bf16[32,3584]{1,0:T(8,128)(2,1)S(1)}, u32[]{:S(2)}, u32[]{:S(2)}) collective-permute-start(bf16[32,3584]{1,0:T(8,128)(2,1)S(1)} %pad_maximum_fusion.6), channel_id=1, source_target_pairs={{0,4},{1,5},{2,3},{3,2},{4,0},{5,1},{6,7},{7,6},{8,12},{9,13},{10,... | collective-permute-start | bytes 688136 | tf_op jit(solution)/shard_map/rows_0_2/ppermute | solution.py:108
  17.5 12.8 %copy-start.6 = (bf16[1,3584,512]{2,1,0:T(8,128)(2,1)S(1)}, bf16[1,3584,512]{2,1,0:T(8,128)(2,1)}, u32[]{:S(2)}) copy-start(bf16[1,3584,512]{2,1,0:T(8,128)(2,1)} %param.12) | copy-start | bytes 11010052
  17.6 8.6 %collective-permute-start.6 = (bf16[32,3712]{1,0:T(8,128)(2,1)S(1)}, bf16[32,3712]{1,0:T(8,128)(2,1)S(1)}, u32[]{:S(2)}, u32[]{:S(2)}) collective-permute-start(bf16[32,3712]{1,0:T(8,128)(2,1)S(1)} %pad_maximum_fusion.5), channel_id=1, source_target_pairs={{0,4},{1,5},{2,3},{3,2},{4,0},{5,1},{6,7},{7,6},{8,12},{9,13},{10,... | collective-permute-start | bytes 712712 | tf_op jit(solution)/shard_map/rows_1_2/ppermute | solution.py:108
  21.6 8.5 %collective-permute-start.3 = (bf16[64,3584]{1,0:T(8,128)(2,1)S(1)}, bf16[64,3584]{1,0:T(8,128)(2,1)S(1)}, u32[]{:S(2)}, u32[]{:S(2)}) collective-permute-start(bf16[64,3584]{1,0:T(8,128)(2,1)S(1)} %pad_maximum_fusion.2), channel_id=1, source_target_pairs={{0,1},{1,0},{2,6},{3,7},{4,5},{5,4},{6,2},{7,3},{8,9},{9,8},{10,14... | collective-permute-start | bytes 1376264 | tf_op jit(solution)/shard_map/rows_0_3/ppermute | solution.py:108
  26.3 9.1 %collective-permute-start.7 = (bf16[64,3712]{1,0:T(8,128)(2,1)S(1)}, bf16[64,3712]{1,0:T(8,128)(2,1)S(1)}, u32[]{:S(2)}, u32[]{:S(2)}) collective-permute-start(bf16[64,3712]{1,0:T(8,128)(2,1)S(1)} %pad_maximum_fusion.1), channel_id=1, source_target_pairs={{0,1},{1,0},{2,6},{3,7},{4,5},{5,4},{6,2},{7,3},{8,9},{9,8},{10,14... | collective-permute-start | bytes 1425416 | tf_op jit(solution)/shard_map/rows_1_3/ppermute | solution.py:108
  30.2 2.0 %copy-start = (bf16[1,1024,1792]{2,1,0:T(8,128)(2,1)S(1)}, bf16[1,1024,1792]{2,1,0:T(8,128)(2,1)}, u32[]{:S(2)}) copy-start(bf16[1,1024,1792]{2,1,0:T(8,128)(2,1)} %param.13) | copy-start | bytes 11010052
  30.2 6.7 %collective-permute-start.8 = (bf16[128,3584]{1,0:T(8,128)(2,1)S(1)}, bf16[128,3584]{1,0:T(8,128)(2,1)S(1)}, u32[]{:S(2)}, u32[]{:S(2)}) collective-permute-start(bf16[128,3584]{1,0:T(8,128)(2,1)S(1)} %constant_dynamic-update-slice_fusion), channel_id=1, source_target_pairs={{0,2},{1,3},{2,0},{3,1},{4,6},{5,7},{6,4},{7,5},{8,10},{9,11},{10,... | collective-permute-start | bytes 2752520 | tf_op jit(solution)/shard_map/rows_0_core/ppermute | solution.py:108
  35.5 4.7 %collective-permute-start.10 = (bf16[128,3712]{1,0:T(8,128)(2,1)S(1)}, bf16[128,3712]{1,0:T(8,128)(2,1)S(1)}, u32[]{:S(2)}, u32[]{:S(2)}) collective-permute-start(bf16[128,3712]{1,0:T(8,128)(2,1)S(1)} %pad_maximum_fusion), channel_id=1, source_target_pairs={{0,2},{1,3},{2,0},{3,1},{4,6},{5,7},{6,4},{7,5},{8,10},{9,11},{10,... | collective-permute-start | bytes 2850824 | tf_op jit(solution)/shard_map/rows_1_core/ppermute | solution.py:108
  36.3 1.3 %copy-start.3 = (bf16[8,3712]{1,0:T(8,128)(2,1)}, bf16[8,3712]{1,0:T(8,128)(2,1)S(1)}, u32[]{:S(2)}) copy-start(bf16[8,3712]{1,0:T(8,128)(2,1)S(1)} %slice_select_fusion.2) | copy-start | bytes 178180
  37.7 9.2 %collective-permute-start.9 = (bf16[256,512]{1,0:T(8,128)(2,1)S(1)}, bf16[256,512]{1,0:T(8,128)(2,1)S(1)}, u32[]{:S(2)}, u32[]{:S(2)}) collective-permute-start(bf16[256,512]{1,0:T(8,128)(2,1)S(1)} %pad_maximum_fusion.3), channel_id=1, source_target_pairs={{0,1},{1,0},{2,3},{3,2},{4,5},{5,4},{6,7},{7,6},{8,9},{9,8},{10,11... | collective-permute-start | bytes 786440 | tf_op jit(solution)/shard_map/acts_0/ppermute | solution.py:108
  41.1 11.3 %collective-permute-start.15 = (bf16[256,512]{1,0:T(8,128)(2,1)S(1)}, bf16[256,512]{1,0:T(8,128)(2,1)S(1)}, u32[]{:S(2)}, u32[]{:S(2)}) collective-permute-start(bf16[256,512]{1,0:T(8,128)(2,1)S(1)} %pad_maximum_fusion.4), channel_id=1, source_target_pairs={{0,1},{1,0},{2,3},{3,2},{4,5},{5,4},{6,7},{7,6},{8,9},{9,8},{10,11... | collective-permute-start | bytes 786440 | tf_op jit(solution)/shard_map/acts_1/ppermute | solution.py:108
  47.4 5.5 %collective-permute-start.11 = (bf16[128,1792]{1,0:T(8,128)(2,1)S(1)}, bf16[128,1792]{1,0:T(8,128)(2,1)S(1)}, u32[]{:S(2)}, u32[]{:S(2)}) collective-permute-start(bf16[128,1792]{1,0:T(8,128)(2,1)S(1)} %fusion.15), channel_id=1, source_target_pairs={{0,2},{1,3},{2,0},{3,1},{4,6},{5,7},{6,4},{7,5},{8,10},{9,11},{10,... | collective-permute-start | bytes 1376264 | tf_op jit(solution)/shard_map/sums_0_core/ppermute | solution.py:108
  52.9 2.7 %collective-permute-start.16 = (bf16[128,1792]{1,0:T(8,128)(2,1)S(1)}, bf16[128,1792]{1,0:T(8,128)(2,1)S(1)}, u32[]{:S(2)}, u32[]{:S(2)}) collective-permute-start(bf16[128,1792]{1,0:T(8,128)(2,1)S(1)} %fusion.23), channel_id=1, source_target_pairs={{0,2},{1,3},{2,0},{3,1},{4,6},{5,7},{6,4},{7,5},{8,10},{9,11},{10,... | collective-permute-start | bytes 1376264 | tf_op jit(solution)/shard_map/sums_1_core/ppermute | solution.py:108
  53.7 6.1 %collective-permute-start.12 = (bf16[64,1792]{1,0:T(8,128)(2,1)S(1)}, bf16[64,1792]{1,0:T(8,128)(2,1)S(1)}, u32[]{:S(2)}, u32[]{:S(2)}) collective-permute-start(bf16[64,1792]{1,0:T(8,128)(2,1)S(1)} %fusion.39), channel_id=1, source_target_pairs={{0,4},{1,5},{2,10},{3,11},{4,0},{5,1},{6,14},{7,15},{8,12},{9,13},... | collective-permute-start | bytes 688136 | tf_op jit(solution)/shard_map/sums_0_0/ppermute | solution.py:108
  56.3 6.2 %collective-permute-start.17 = (bf16[64,1792]{1,0:T(8,128)(2,1)S(1)}, bf16[64,1792]{1,0:T(8,128)(2,1)S(1)}, u32[]{:S(2)}, u32[]{:S(2)}) collective-permute-start(bf16[64,1792]{1,0:T(8,128)(2,1)S(1)} %fusion.41), channel_id=1, source_target_pairs={{0,4},{1,5},{2,10},{3,11},{4,0},{5,1},{6,14},{7,15},{8,12},{9,13},... | collective-permute-start | bytes 688136 | tf_op jit(solution)/shard_map/sums_1_0/ppermute | solution.py:108
  59.9 4.9 %collective-permute-start.13 = (bf16[32,1792]{1,0:T(8,128)(2,1)S(1)}, bf16[32,1792]{1,0:T(8,128)(2,1)S(1)}, u32[]{:S(2)}, u32[]{:S(2)}) collective-permute-start(bf16[32,1792]{1,0:T(8,128)(2,1)S(1)} %bitcast.81), channel_id=1, source_target_pairs={{0,8},{1,9},{2,6},{3,7},{4,12},{5,13},{6,2},{7,3},{8,0},{9,1},{10,... | collective-permute-start | bytes 344072 | tf_op jit(solution)/shard_map/sums_0_1/ppermute | solution.py:108
  62.6 13.0 %copy-start.2 = (bf16[16,3584]{1,0:T(8,128)(2,1)S(1)}, bf16[16,3584]{1,0:T(8,128)(2,1)}, u32[]{:S(2)}) copy-start(bf16[16,3584]{1,0:T(8,128)(2,1)} %param.9) | copy-start | bytes 344068
  62.6 13.0 %slice-start = ((bf16[8,3712]{1,0:T(8,128)(2,1)}), bf16[8,3584]{1,0:T(8,128)(2,1)S(1)}, s32[]{:S(2)}) async-start(bf16[8,3712]{1,0:T(8,128)(2,1)} %copy-done.3), calls=%async_computation | async-start | bytes 114688 | tf_op jit(solution)/shard_map/slice | solution.py:243
  62.6 14.6 %copy-start.4 = (bf16[8,3712]{1,0:T(8,128)(2,1)S(1)}, bf16[8,3712]{1,0:T(8,128)(2,1)}, u32[]{:S(2)}) copy-start(bf16[8,3712]{1,0:T(8,128)(2,1)} %copy-done.3) | copy-start | bytes 178180
  62.7 7.1 %collective-permute-start.18 = (bf16[32,1792]{1,0:T(8,128)(2,1)S(1)}, bf16[32,1792]{1,0:T(8,128)(2,1)S(1)}, u32[]{:S(2)}, u32[]{:S(2)}) collective-permute-start(bf16[32,1792]{1,0:T(8,128)(2,1)S(1)} %bitcast.82), channel_id=1, source_target_pairs={{0,8},{1,9},{2,6},{3,7},{4,12},{5,13},{6,2},{7,3},{8,0},{9,1},{10,... | collective-permute-start | bytes 344072 | tf_op jit(solution)/shard_map/sums_1_1/ppermute | solution.py:108
  64.7 16.2 %copy-start.5 = (f32[3584]{0:T(1024)S(1)}, f32[3584]{0:T(1024)}, u32[]{:S(2)}) copy-start(f32[3584]{0:T(1024)} %param.17) | copy-start | bytes 43012
  64.8 8.7 %collective-permute-start.14 = (bf16[16,1792]{1,0:T(8,128)(2,1)S(1)}, bf16[16,1792]{1,0:T(8,128)(2,1)S(1)}, u32[]{:S(2)}, u32[]{:S(2)}) collective-permute-start(bf16[16,1792]{1,0:T(8,128)(2,1)S(1)} %fusion.76), channel_id=1, source_target_pairs={{0,16},{1,17},{2,18},{3,19},{4,20},{5,21},{6,22},{7,23},{8,24},{9,... | collective-permute-start | bytes 172040 | tf_op jit(solution)/shard_map/sums_0_2/ppermute | solution.py:108
  69.8 5.8 %collective-permute-start.19 = (bf16[16,1792]{1,0:T(8,128)(2,1)S(1)}, bf16[16,1792]{1,0:T(8,128)(2,1)S(1)}, u32[]{:S(2)}, u32[]{:S(2)}) collective-permute-start(bf16[16,1792]{1,0:T(8,128)(2,1)S(1)} %fusion.77), channel_id=1, source_target_pairs={{0,16},{1,17},{2,18},{3,19},{4,20},{5,21},{6,22},{7,23},{8,24},{9,... | collective-permute-start | bytes 172040 | tf_op jit(solution)/shard_map/sums_1_2/ppermute | solution.py:108
  75.7 4.9 %collective-permute-start.20 = (bf16[32,1792]{1,0:T(8,128)(2,1)S(1)}, bf16[32,1792]{1,0:T(8,128)(2,1)S(1)}, u32[]{:S(2)}, u32[]{:S(2)}) collective-permute-start(bf16[32,1792]{1,0:T(8,128)(2,1)S(1)} %fusion.54), channel_id=1, source_target_pairs={{0,1},{1,0},{2,3},{3,2},{4,5},{5,4},{6,7},{7,6},{8,9},{9,8},{10,11... | collective-permute-start | bytes 344072 | tf_op jit(solution)/shard_map/layer/ppermute | solution.py:108
  80.6 1.0 %copy-start.1 = (bf16[16,3584]{1,0:T(8,128)(2,1)}, bf16[16,3584]{1,0:T(8,128)(2,1)S(1)}, u32[]{:S(2)}) copy-start(bf16[16,3584]{1,0:T(8,128)(2,1)S(1)} %slice.591) | copy-start | bytes 344068

commit v3 on v2

--- a/solution.py
+++ b/solution.py
@@ -1,6 +1,8 @@
 import jax
 import jax.numpy as jnp
 from jax import lax
+from jax.experimental import pallas as pl
+from jax.experimental.pallas import tpu as pltpu
 from jax.sharding import PartitionSpec as P
 
 
@@ -108,12 +110,44 @@
         return lax.ppermute(array, ("expert", "req"), pairs)
 
 
-def three_parts(value):
-    first = value.astype(jnp.bfloat16)
-    rest = value - first.astype(jnp.float32)
-    second = rest.astype(jnp.bfloat16)
-    third = (rest - second.astype(jnp.float32)).astype(jnp.bfloat16)
-    return [first, second, third]
+def beside_kernel(count_ref, pos_ref, ids_ref, route_ref, out_ref):
+    top_k, tree_len = ids_ref.shape
+    half, wide = tree_len // 2, out_ref.shape[1]
+    expert = lax.broadcasted_iota(jnp.int32, (tree_len, tree_len), 0)
+    dense = jnp.zeros((tree_len, tree_len), jnp.float32)
+    for k in range(top_k):
+        dense = jnp.where(expert == ids_ref[k : k + 1], route_ref[k : k + 1], dense)
+    row = lax.broadcasted_iota(jnp.int32, (tree_len, wide), 0)
+    column = lax.broadcasted_iota(jnp.int32, (tree_len, wide), 1)
+    sides = [jnp.zeros((tree_len, wide), jnp.float32) for _ in range(2)]
+    for part in range(3):
+        rounded = dense.astype(jnp.bfloat16)
+        dense = dense - rounded.astype(jnp.float32)
+        for k in range(2):
+            spread = column == row + (part * tree_len + k * wide // 2)
+            sides[k] += lax.dot_general(
+                rounded,
+                spread.astype(jnp.bfloat16),
+                (((0,), (0,)), ((), ())),
+                preferred_element_type=jnp.float32,
+            )
+    both = sides[0][:half] + sides[1][half:]
+    for a in range(pos_ref.shape[1]):
+        at = (a // half) * (wide // 2) + 3 * tree_len + pos_ref[0, a]
+        hit = (row[:half] == a % half) & (column[:half] == at) & (a < count_ref[0])
+        both = jnp.where(hit, 1.0, both)
+    out_ref[...] = both.astype(jnp.bfloat16)
+
+
+def beside(expert_ids, route_weights, accept_count, accept_pos):
+    vmem, smem = pl.BlockSpec(memory_space=pltpu.VMEM), pl.BlockSpec(memory_space=pltpu.SMEM)
+    return pl.pallas_call(
+        beside_kernel,
+        out_shape=jax.ShapeDtypeStruct((expert_ids.shape[0] // 2, 128), jnp.bfloat16),
+        in_specs=[smem, smem, vmem, vmem],
+        out_specs=vmem,
+        name="beside_rows",
+    )(accept_count, accept_pos, expert_ids.T, route_weights.T)
 
 
 def blocks_of(array, order, length):
@@ -143,18 +177,10 @@
     half = tree_len // 2
 
     experts = jnp.arange(expert_count, dtype=jnp.int32)
-    dense = jnp.sum(
-        jnp.where(expert_ids[:, :, None] == experts[None, None, :], route_weights[:, :, None], 0.0),
-        axis=1,
-    )
-    selector = selector_of(accept_pos, accept_count, tree_len)
-    selector = jnp.pad(selector, ((0, tree_len - accept_len), (0, 0)))
-    extra = jnp.concatenate(three_parts(dense) + [selector], axis=1)
-    width = extra.shape[1]
-    extra = jnp.concatenate([extra[:half], extra[half:]], axis=1)
-    extra = jnp.pad(extra, ((0, 0), (0, -extra.shape[1] % 128)))
+    width = 64
 
     there = swap(tree_hidden, "rows", FAR, NEAR)
+    extra = beside(expert_ids, route_weights, accept_count, accept_pos)
     extra_there = swap(extra, "extra", FAR, NEAR)
     blocks = [
         jnp.concatenate([tree_hidden[:half], there[:half]], axis=0),
@@ -200,7 +226,8 @@
 
     acts, acts_there = [], []
     for k in range(2):
-        acts.append((up(own[k]), up(other[k])))
+        both = up(jnp.concatenate([own[k][:, :features], other[k][:, :features]], axis=0))
+        acts.append((both[:span], both[span:]))
         turned = (
             jnp.where(first_core, last(acts[k][0]), last_but_one(acts[k][0])),
             jnp.where(first_core, last_but_one(acts[k][1]), last(acts[k][1])),
@@ -253,8 +280,9 @@
     stays = draft_owner[0] == side
     chosen = jnp.where(stays, layer_local, layer_pair[tree_len:])
     at = features + 3 * expert_count
-    there = jnp.concatenate([second[1][:, at : at + tree_len], second[1][:, at + width : at + width + tree_len]], axis=0)
-    chosen_selector = jnp.where(stays, selector, there)[:accept_len]
+    own_beside = extra[:, at - features : at - features + tree_len]
+    there_beside = second[1][:, at : at + tree_len]
+    chosen_selector = jnp.where(stays, own_beside, there_beside)[:accept_len]
     incoming = jnp.dot(chosen_selector, chosen, preferred_element_type=jnp.float32)
     return (layer_local, norm_rows(incoming, mtp_gain))
 
@@ -264,7 +292,7 @@
         tree_len, top_k = arrays[1].shape
         expert_count = mesh.shape["expert"]
         whole = capacity_of(tree_len, top_k, expert_count) == tree_len
-        if whole and expert_count == 16 and mesh.shape["req"] == 2:
+        if whole and tree_len == expert_count == 16 and mesh.shape["req"] == 2:
             return gathered_plan(*arrays)
         return routed_plan(*arrays)
 

time: 81.9 us -> 79.1 us (0.966)
  starting transfers between devices: 32.4 us -> 28.5 us
  Pallas kernels: 0 us -> 1.5 us
  waiting for transfers between devices: 32.5 us -> 33.8 us
  local copies, waits for them, and re-layouts: 4.26 us -> 3.44 us
    ppermute x21, starting transfers between devices: 32.4 us -> 28.5 us  [swap(): return lax.ppermute(array, ('expert', 'req'), pairs)]
    pallas_call x0 -> x1, Pallas kernels: none -> 1.5 us  [beside(): pl.pallas_call(beside_kernel, out_shape=jax.ShapeDtypeStruct((expert_ids....]
    ppermute x21, waiting for transfers between devices: 32.5 us -> 33.8 us  [swap(): return lax.ppermute(array, ('expert', 'req'), pairs)]
    slice x4 -> x2, local copies, waits for them, and re-layouts: 0.95 us -> 0.12 us  [the longest x1 0.06 us: gathered_plan(): own[k][:, :features]]
    dot_general x4 -> x2, matrix products: 2.77 us -> 2.37 us  [up(): jnp.dot(part[:, :features], w_up[0], preferred_element_type=jnp.float32)]
    unnamed x46 -> x48, local copies, waits for them, and re-layouts: 2.94 us -> 2.86 us
  transfers between devices with their start and end apart: 21 -> 21, of which waited for: 14 -> 12; matrix products, arithmetic and copies ran while one was open for 14% -> 12% of each run, Pallas kernels for 0% -> 2%
where the time goes in v3:
time: 79.1 us; the launch traced here: 78.8 us
  waiting for transfers between devices  33.8 us (43%)
  starting transfers between devices  28.5 us (36%)
  matrix products  6.13 us (8%)
  local copies, waits for them, and re-layouts  3.44 us (4%)
  between operations  2.75 us (3%)
  other arithmetic  2.71 us (3%)
  Pallas kernels  1.5 us (2%)
    ppermute x21, waiting for transfers between devices, swap(): return lax.ppermute(array, ('expert', 'req'), pairs)  33.8 us
    ppermute x21, starting transfers between devices, swap(): return lax.ppermute(array, ('expert', 'req'), pairs)  28.5 us
    unnamed x48, local copies, waits for them, and re-layouts  2.86 us
    dot_general x2, matrix products, up(): jnp.dot(part[:, :features], w_up[0], preferred_element_type=jnp.float32)  2.37 us
    dot_general x4, matrix products, down(): jnp.dot(acts_there, w_other, preferred_element_type=jnp.float32)  1.76 us
    dot_general x4, matrix products, down(): jnp.dot(acts_here, w_own, preferred_element_type=jnp.float32)  1.68 us
  transfers between devices with their start and end apart: 21, of which 12 were waited for; matrix products, arithmetic and copies ran while one was open for 12% of the time, Pallas kernels for 2%

profile of v3, /device:TPU:0, one launch (start us, length us, event | category | flops | bytes accessed | tf_op | source)
XLA Modules:
  0.0 78.8 jit_solution(12562488593928329280)
XLA Ops:
  0.6 4.1 %collective-permute-start = (bf16[16,3584]{1,0:T(8,128)(2,1)}, bf16[16,3584]{1,0:T(8,128)(2,1)S(1)}, u32[]{:S(2)}, u32[]{:S(2)}) collective-permute-start(bf16[16,3584]{1,0:T(8,128)(2,1)} %param.9), channel_id=1, source_target_pairs={{0,16},{1,17},{2,10},{3,11},{4,20},{5,21},{6,14},{7,15},{8,24},{9,... | collective-permute-start | bytes 344072 | tf_op jit(solution)/shard_map/rows/ppermute | solution.py:110
  5.4 1.5 %beside_rows.1 = bf16[8,128]{1,0:T(8,128)(2,1)} custom-call(s32[1]{0:T(128)S(6)} %copy.48.count_ref, s32[1,8]{1,0:T(1,128)} %pos_ref.1, s32[8,16]{1,0:T(8,128)} %bitcast.69, f32[8,16]{1,0:T(8,128)} %bitcast.70), custom_call_target="tpu_custom_call" | custom-call | tf_op jit(solution)/shard_map/beside_rows/pallas_call | solution.py:144
  6.9 0.9 %constant_dynamic-update-slice_fusion.4 = (bf16[128,3584]{1,0:T(8,128)(2,1)S(1)}, bf16[256,3584]{1,0:T(8,128)(2,1)S(1)}, bf16[8,3584]{1,0:T(8,128)(2,1)S(1)}, bf16[8,3584]{1,0:T(8,128)(2,1)S(1)}) fusion(bf16[16,3584]{1,0:T(8,128)(2,1)} %param.9), kind=kLoop, calls=%fused_computation.100 | loop fusion | bytes 344064
  7.8 2.4 %collective-permute-start.1 = (bf16[16,3584]{1,0:T(8,128)(2,1)S(1)}, bf16[16,3584]{1,0:T(8,128)(2,1)S(1)}, u32[]{:S(2)}, u32[]{:S(2)}) collective-permute-start(bf16[16,3584]{1,0:T(8,128)(2,1)S(1)} %pad_maximum_fusion.8), channel_id=1, source_target_pairs={{0,8},{1,9},{2,18},{3,19},{4,12},{5,13},{6,22},{7,23},{8,0},{9,1},... | collective-permute-start | bytes 344072 | tf_op jit(solution)/shard_map/rows_0_1/ppermute | solution.py:110
  10.2 2.4 %collective-permute-done.4 = bf16[8,128]{1,0:T(8,128)(2,1)S(1)} collective-permute-done((bf16[8,128]{1,0:T(8,128)(2,1)}, bf16[8,128]{1,0:T(8,128)(2,1)S(1)}, u32[]{:S(2)}, u32[]{:S(2)}) %collective-permute-start.4) | collective-permute-done | bytes 2080 | tf_op jit(solution)/shard_map/extra/ppermute | solution.py:110
  12.6 0.7 maximum_maximum_fusion
  13.9 2.0 %collective-permute-start.2 = (bf16[32,3584]{1,0:T(8,128)(2,1)S(1)}, bf16[32,3584]{1,0:T(8,128)(2,1)S(1)}, u32[]{:S(2)}, u32[]{:S(2)}) collective-permute-start(bf16[32,3584]{1,0:T(8,128)(2,1)S(1)} %pad_maximum_fusion.6), channel_id=1, source_target_pairs={{0,4},{1,5},{2,3},{3,2},{4,0},{5,1},{6,7},{7,6},{8,12},{9,13},{10,... | collective-permute-start | bytes 688136 | tf_op jit(solution)/shard_map/rows_0_2/ppermute | solution.py:110
  16.0 2.2 %collective-permute-done.5 = bf16[16,3712]{1,0:T(8,128)(2,1)S(1)} collective-permute-done((bf16[16,3712]{1,0:T(8,128)(2,1)S(1)}, bf16[16,3712]{1,0:T(8,128)(2,1)S(1)}, u32[]{:S(2)}, u32[]{:S(2)}) %collective-permute-start.5) | collective-permute-done | bytes 118816 | tf_op jit(solution)/shard_map/rows_1_1/ppermute | solution.py:110
  18.3 1.6 %collective-permute-start.6 = (bf16[32,3712]{1,0:T(8,128)(2,1)S(1)}, bf16[32,3712]{1,0:T(8,128)(2,1)S(1)}, u32[]{:S(2)}, u32[]{:S(2)}) collective-permute-start(bf16[32,3712]{1,0:T(8,128)(2,1)S(1)} %pad_maximum_fusion.5), channel_id=1, source_target_pairs={{0,4},{1,5},{2,3},{3,2},{4,0},{5,1},{6,7},{7,6},{8,12},{9,13},{10,... | collective-permute-start | bytes 712712 | tf_op jit(solution)/shard_map/rows_1_2/ppermute | solution.py:110
  20.1 2.0 %collective-permute-start.3 = (bf16[64,3584]{1,0:T(8,128)(2,1)S(1)}, bf16[64,3584]{1,0:T(8,128)(2,1)S(1)}, u32[]{:S(2)}, u32[]{:S(2)}) collective-permute-start(bf16[64,3584]{1,0:T(8,128)(2,1)S(1)} %pad_maximum_fusion.2), channel_id=1, source_target_pairs={{0,1},{1,0},{2,6},{3,7},{4,5},{5,4},{6,2},{7,3},{8,9},{9,8},{10,14... | collective-permute-start | bytes 1376264 | tf_op jit(solution)/shard_map/rows_0_3/ppermute | solution.py:110
  22.1 5.0 %collective-permute-done.6 = bf16[32,3712]{1,0:T(8,128)(2,1)S(1)} collective-permute-done((bf16[32,3712]{1,0:T(8,128)(2,1)S(1)}, bf16[32,3712]{1,0:T(8,128)(2,1)S(1)}, u32[]{:S(2)}, u32[]{:S(2)}) %collective-permute-start.6) | collective-permute-done | bytes 237600 | tf_op jit(solution)/shard_map/rows_1_2/ppermute | solution.py:110
  27.1 1.5 %collective-permute-start.7 = (bf16[64,3712]{1,0:T(8,128)(2,1)S(1)}, bf16[64,3712]{1,0:T(8,128)(2,1)S(1)}, u32[]{:S(2)}, u32[]{:S(2)}) collective-permute-start(bf16[64,3712]{1,0:T(8,128)(2,1)S(1)} %pad_maximum_fusion.1), channel_id=1, source_target_pairs={{0,1},{1,0},{2,6},{3,7},{4,5},{5,4},{6,2},{7,3},{8,9},{9,8},{10,14... | collective-permute-start | bytes 1425416 | tf_op jit(solution)/shard_map/rows_1_3/ppermute | solution.py:110
  28.8 7.0 %collective-permute-done.7 = bf16[64,3712]{1,0:T(8,128)(2,1)S(1)} collective-permute-done((bf16[64,3712]{1,0:T(8,128)(2,1)S(1)}, bf16[64,3712]{1,0:T(8,128)(2,1)S(1)}, u32[]{:S(2)}, u32[]{:S(2)}) %collective-permute-start.7) | collective-permute-done | bytes 475168 | tf_op jit(solution)/shard_map/rows_1_3/ppermute | solution.py:110
  36.2 1.7 %copy-done.7 = bf16[1,3584,512]{2,1,0:T(8,128)(2,1)S(1)} copy-done((bf16[1,3584,512]{2,1,0:T(8,128)(2,1)S(1)}, bf16[1,3584,512]{2,1,0:T(8,128)(2,1)}, u32[]{:S(2)}) %copy-start.7) | copy-done | bytes 3670040
  38.0 1.2 %multiply_convert_fusion.1 = bf16[256,512]{1,0:T(8,128)(2,1)S(1)} fusion(bf16[256,3584]{1,0:T(8,128)(2,1)S(1)} %constant_dynamic-update-slice_fusion.5, bf16[1,3584,512]{2,1,0:T(8,128)(2,1)S(1)} %copy-done.7), kind=kOutput, calls=%fused_computation.41 | convolution fusion | flops 940179456 | bytes 5767168 | tf_op jit(solution)/shard_map/dot_general | solution.py:207
  39.3 1.5 %collective-permute-start.9 = (bf16[256,512]{1,0:T(8,128)(2,1)S(1)}, bf16[256,512]{1,0:T(8,128)(2,1)S(1)}, u32[]{:S(2)}, u32[]{:S(2)}) collective-permute-start(bf16[256,512]{1,0:T(8,128)(2,1)S(1)} %pad_maximum_fusion.3), channel_id=1, source_target_pairs={{0,1},{1,0},{2,3},{3,2},{4,5},{5,4},{6,7},{7,6},{8,9},{9,8},{10,11... | collective-permute-start | bytes 786440 | tf_op jit(solution)/shard_map/acts_0/ppermute | solution.py:110
  41.8 1.2 %multiply_convert_fusion = bf16[256,512]{1,0:T(8,128)(2,1)S(1)} fusion(bf16[1,3584,512]{2,1,0:T(8,128)(2,1)S(1)} %copy-done.7, bf16[128,3584]{1,0:T(8,128)(2,1)S(1)} %slice.570, bf16[128,3584]{1,0:T(8,128)(2,1)S(1)} %slice.569), kind=kOutput, calls=%fused_computation.40 | convolution fusion | flops 943849472 | bytes 5767168 | tf_op jit(solution)/shard_map/dot_general | solution.py:207
  44.7 3.8 %collective-permute-done.9 = bf16[256,512]{1,0:T(8,128)(2,1)S(1)} collective-permute-done((bf16[256,512]{1,0:T(8,128)(2,1)S(1)}, bf16[256,512]{1,0:T(8,128)(2,1)S(1)}, u32[]{:S(2)}, u32[]{:S(2)}) %collective-permute-start.9) | collective-permute-done | bytes 262176 | tf_op jit(solution)/shard_map/acts_0/ppermute | solution.py:110
  49.4 2.7 %collective-permute-done.15 = bf16[256,512]{1,0:T(8,128)(2,1)S(1)} collective-permute-done((bf16[256,512]{1,0:T(8,128)(2,1)S(1)}, bf16[256,512]{1,0:T(8,128)(2,1)S(1)}, u32[]{:S(2)}, u32[]{:S(2)}) %collective-permute-start.15) | collective-permute-done | bytes 262176 | tf_op jit(solution)/shard_map/acts_1/ppermute | solution.py:110
  53.3 1.6 %collective-permute-start.12 = (bf16[64,1792]{1,0:T(8,128)(2,1)S(1)}, bf16[64,1792]{1,0:T(8,128)(2,1)S(1)}, u32[]{:S(2)}, u32[]{:S(2)}) collective-permute-start(bf16[64,1792]{1,0:T(8,128)(2,1)S(1)} %fusion.42), channel_id=1, source_target_pairs={{0,4},{1,5},{2,10},{3,11},{4,0},{5,1},{6,14},{7,15},{8,12},{9,13},... | collective-permute-start | bytes 688136 | tf_op jit(solution)/shard_map/sums_0_0/ppermute | solution.py:110
  55.7 1.0 %collective-permute-start.17 = (bf16[64,1792]{1,0:T(8,128)(2,1)S(1)}, bf16[64,1792]{1,0:T(8,128)(2,1)S(1)}, u32[]{:S(2)}, u32[]{:S(2)}) collective-permute-start(bf16[64,1792]{1,0:T(8,128)(2,1)S(1)} %fusion.44), channel_id=1, source_target_pairs={{0,4},{1,5},{2,10},{3,11},{4,0},{5,1},{6,14},{7,15},{8,12},{9,13},... | collective-permute-start | bytes 688136 | tf_op jit(solution)/shard_map/sums_1_0/ppermute | solution.py:110
  56.7 2.6 %collective-permute-done.12 = bf16[64,1792]{1,0:T(8,128)(2,1)S(1)} collective-permute-done((bf16[64,1792]{1,0:T(8,128)(2,1)S(1)}, bf16[64,1792]{1,0:T(8,128)(2,1)S(1)}, u32[]{:S(2)}, u32[]{:S(2)}) %collective-permute-start.12) | collective-permute-done | bytes 229408 | tf_op jit(solution)/shard_map/sums_0_0/ppermute | solution.py:110
  59.5 0.8 %collective-permute-start.13 = (bf16[32,1792]{1,0:T(8,128)(2,1)S(1)}, bf16[32,1792]{1,0:T(8,128)(2,1)S(1)}, u32[]{:S(2)}, u32[]{:S(2)}) collective-permute-start(bf16[32,1792]{1,0:T(8,128)(2,1)S(1)} %bitcast.67), channel_id=1, source_target_pairs={{0,8},{1,9},{2,6},{3,7},{4,12},{5,13},{6,2},{7,3},{8,0},{9,1},{10,... | collective-permute-start | bytes 344072 | tf_op jit(solution)/shard_map/sums_0_1/ppermute | solution.py:110
  60.3 1.5 %collective-permute-done.17 = bf16[64,1792]{1,0:T(8,128)(2,1)S(1)} collective-permute-done((bf16[64,1792]{1,0:T(8,128)(2,1)S(1)}, bf16[64,1792]{1,0:T(8,128)(2,1)S(1)}, u32[]{:S(2)}, u32[]{:S(2)}) %collective-permute-start.17) | collective-permute-done | bytes 229408 | tf_op jit(solution)/shard_map/sums_1_0/ppermute | solution.py:110
  62.0 0.8 %collective-permute-start.18 = (bf16[32,1792]{1,0:T(8,128)(2,1)S(1)}, bf16[32,1792]{1,0:T(8,128)(2,1)S(1)}, u32[]{:S(2)}, u32[]{:S(2)}) collective-permute-start(bf16[32,1792]{1,0:T(8,128)(2,1)S(1)} %bitcast.68), channel_id=1, source_target_pairs={{0,8},{1,9},{2,6},{3,7},{4,12},{5,13},{6,2},{7,3},{8,0},{9,1},{10,... | collective-permute-start | bytes 344072 | tf_op jit(solution)/shard_map/sums_1_1/ppermute | solution.py:110
  62.8 1.5 %collective-permute-done.13 = bf16[32,1792]{1,0:T(8,128)(2,1)S(1)} collective-permute-done((bf16[32,1792]{1,0:T(8,128)(2,1)S(1)}, bf16[32,1792]{1,0:T(8,128)(2,1)S(1)}, u32[]{:S(2)}, u32[]{:S(2)}) %collective-permute-start.13) | collective-permute-done | bytes 114720 | tf_op jit(solution)/shard_map/sums_0_1/ppermute | solution.py:110
  64.4 3.1 %collective-permute-start.14 = (bf16[16,1792]{1,0:T(8,128)(2,1)S(1)}, bf16[16,1792]{1,0:T(8,128)(2,1)S(1)}, u32[]{:S(2)}, u32[]{:S(2)}) collective-permute-start(bf16[16,1792]{1,0:T(8,128)(2,1)S(1)} %fusion.71), channel_id=1, source_target_pairs={{0,16},{1,17},{2,18},{3,19},{4,20},{5,21},{6,22},{7,23},{8,24},{9,... | collective-permute-start | bytes 172040 | tf_op jit(solution)/shard_map/sums_0_2/ppermute | solution.py:110
  67.5 3.1 %collective-permute-start.19 = (bf16[16,1792]{1,0:T(8,128)(2,1)S(1)}, bf16[16,1792]{1,0:T(8,128)(2,1)S(1)}, u32[]{:S(2)}, u32[]{:S(2)}) collective-permute-start(bf16[16,1792]{1,0:T(8,128)(2,1)S(1)} %fusion.72), channel_id=1, source_target_pairs={{0,16},{1,17},{2,18},{3,19},{4,20},{5,21},{6,22},{7,23},{8,24},{9,... | collective-permute-start | bytes 172040 | tf_op jit(solution)/shard_map/sums_1_2/ppermute | solution.py:110
  70.6 2.1 %collective-permute-done.19 = bf16[16,1792]{1,0:T(8,128)(2,1)S(1)} collective-permute-done((bf16[16,1792]{1,0:T(8,128)(2,1)S(1)}, bf16[16,1792]{1,0:T(8,128)(2,1)S(1)}, u32[]{:S(2)}, u32[]{:S(2)}) %collective-permute-start.19) | collective-permute-done | bytes 57376 | tf_op jit(solution)/shard_map/sums_1_2/ppermute | solution.py:110
  72.8 1.6 %collective-permute-start.20 = (bf16[32,1792]{1,0:T(8,128)(2,1)S(1)}, bf16[32,1792]{1,0:T(8,128)(2,1)S(1)}, u32[]{:S(2)}, u32[]{:S(2)}) collective-permute-start(bf16[32,1792]{1,0:T(8,128)(2,1)S(1)} %fusion.45), channel_id=1, source_target_pairs={{0,1},{1,0},{2,3},{3,2},{4,5},{5,4},{6,7},{7,6},{8,9},{9,8},{10,11... | collective-permute-start | bytes 344072 | tf_op jit(solution)/shard_map/layer/ppermute | solution.py:110
  75.0 2.6 %collective-permute-done.20 = bf16[32,1792]{1,0:T(8,128)(2,1)S(1)} collective-permute-done((bf16[32,1792]{1,0:T(8,128)(2,1)S(1)}, bf16[32,1792]{1,0:T(8,128)(2,1)S(1)}, u32[]{:S(2)}, u32[]{:S(2)}) %collective-permute-start.20) | collective-permute-done | bytes 114720 | tf_op jit(solution)/shard_map/layer/ppermute | solution.py:110
  78.1 0.7 fusion.70
  (126 shorter events, 7.7 us)
Async XLA Ops:
  0.6 7.2 %collective-permute-start = (bf16[16,3584]{1,0:T(8,128)(2,1)}, bf16[16,3584]{1,0:T(8,128)(2,1)S(1)}, u32[]{:S(2)}, u32[]{:S(2)}) collective-permute-start(bf16[16,3584]{1,0:T(8,128)(2,1)} %param.9), channel_id=1, source_target_pairs={{0,16},{1,17},{2,10},{3,11},{4,20},{5,21},{6,14},{7,15},{8,24},{9,... | collective-permute-start | bytes 344072 | tf_op jit(solution)/shard_map/rows/ppermute | solution.py:110
  6.9 11.4 %copy-start.5 = (bf16[8,128]{1,0:T(8,128)(2,1)S(1)}, bf16[8,128]{1,0:T(8,128)(2,1)}, u32[]{:S(2)}) copy-start(bf16[8,128]{1,0:T(8,128)(2,1)} %beside_rows.1) | copy-start | bytes 6148
  6.9 5.8 %collective-permute-start.4 = (bf16[8,128]{1,0:T(8,128)(2,1)}, bf16[8,128]{1,0:T(8,128)(2,1)S(1)}, u32[]{:S(2)}, u32[]{:S(2)}) collective-permute-start(bf16[8,128]{1,0:T(8,128)(2,1)} %beside_rows.1), channel_id=1, source_target_pairs={{0,16},{1,17},{2,10},{3,11},{4,20},{5,21},{6,14},{7,15},{8,24},{9,... | collective-permute-start | bytes 6152 | tf_op jit(solution)/shard_map/extra/ppermute | solution.py:110
  7.8 6.1 %collective-permute-start.1 = (bf16[16,3584]{1,0:T(8,128)(2,1)S(1)}, bf16[16,3584]{1,0:T(8,128)(2,1)S(1)}, u32[]{:S(2)}, u32[]{:S(2)}) collective-permute-start(bf16[16,3584]{1,0:T(8,128)(2,1)S(1)} %pad_maximum_fusion.8), channel_id=1, source_target_pairs={{0,8},{1,9},{2,18},{3,19},{4,12},{5,13},{6,22},{7,23},{8,0},{9,1},... | collective-permute-start | bytes 344072 | tf_op jit(solution)/shard_map/rows_0_1/ppermute | solution.py:110
  13.3 4.9 %collective-permute-start.5 = (bf16[16,3712]{1,0:T(8,128)(2,1)S(1)}, bf16[16,3712]{1,0:T(8,128)(2,1)S(1)}, u32[]{:S(2)}, u32[]{:S(2)}) collective-permute-start(bf16[16,3712]{1,0:T(8,128)(2,1)S(1)} %maximum_maximum_fusion), channel_id=1, source_target_pairs={{0,8},{1,9},{2,18},{3,19},{4,12},{5,13},{6,22},{7,23},{8,0},{9,1},... | collective-permute-start | bytes 356360 | tf_op jit(solution)/shard_map/rows_1_1/ppermute | solution.py:110
  13.9 6.1 %collective-permute-start.2 = (bf16[32,3584]{1,0:T(8,128)(2,1)S(1)}, bf16[32,3584]{1,0:T(8,128)(2,1)S(1)}, u32[]{:S(2)}, u32[]{:S(2)}) collective-permute-start(bf16[32,3584]{1,0:T(8,128)(2,1)S(1)} %pad_maximum_fusion.6), channel_id=1, source_target_pairs={{0,4},{1,5},{2,3},{3,2},{4,0},{5,1},{6,7},{7,6},{8,12},{9,13},{10,... | collective-permute-start | bytes 688136 | tf_op jit(solution)/shard_map/rows_0_2/ppermute | solution.py:110
  18.3 8.8 %collective-permute-start.6 = (bf16[32,3712]{1,0:T(8,128)(2,1)S(1)}, bf16[32,3712]{1,0:T(8,128)(2,1)S(1)}, u32[]{:S(2)}, u32[]{:S(2)}) collective-permute-start(bf16[32,3712]{1,0:T(8,128)(2,1)S(1)} %pad_maximum_fusion.5), channel_id=1, source_target_pairs={{0,4},{1,5},{2,3},{3,2},{4,0},{5,1},{6,7},{7,6},{8,12},{9,13},{10,... | collective-permute-start | bytes 712712 | tf_op jit(solution)/shard_map/rows_1_2/ppermute | solution.py:110
  20.1 8.6 %collective-permute-start.3 = (bf16[64,3584]{1,0:T(8,128)(2,1)S(1)}, bf16[64,3584]{1,0:T(8,128)(2,1)S(1)}, u32[]{:S(2)}, u32[]{:S(2)}) collective-permute-start(bf16[64,3584]{1,0:T(8,128)(2,1)S(1)} %pad_maximum_fusion.2), channel_id=1, source_target_pairs={{0,1},{1,0},{2,6},{3,7},{4,5},{5,4},{6,2},{7,3},{8,9},{9,8},{10,14... | collective-permute-start | bytes 1376264 | tf_op jit(solution)/shard_map/rows_0_3/ppermute | solution.py:110
  27.1 8.7 %collective-permute-start.7 = (bf16[64,3712]{1,0:T(8,128)(2,1)S(1)}, bf16[64,3712]{1,0:T(8,128)(2,1)S(1)}, u32[]{:S(2)}, u32[]{:S(2)}) collective-permute-start(bf16[64,3712]{1,0:T(8,128)(2,1)S(1)} %pad_maximum_fusion.1), channel_id=1, source_target_pairs={{0,1},{1,0},{2,6},{3,7},{4,5},{5,4},{6,2},{7,3},{8,9},{9,8},{10,14... | collective-permute-start | bytes 1425416 | tf_op jit(solution)/shard_map/rows_1_3/ppermute | solution.py:110
  28.7 7.5 %collective-permute-start.8 = (bf16[128,3584]{1,0:T(8,128)(2,1)S(1)}, bf16[128,3584]{1,0:T(8,128)(2,1)S(1)}, u32[]{:S(2)}, u32[]{:S(2)}) collective-permute-start(bf16[128,3584]{1,0:T(8,128)(2,1)S(1)} %get-tuple-element.18), channel_id=1, source_target_pairs={{0,2},{1,3},{2,0},{3,1},{4,6},{5,7},{6,4},{7,5},{8,10},{9,11},{10,... | collective-permute-start | bytes 2752520 | tf_op jit(solution)/shard_map/rows_0_core/ppermute | solution.py:110
  35.9 2.1 %copy-start.7 = (bf16[1,3584,512]{2,1,0:T(8,128)(2,1)S(1)}, bf16[1,3584,512]{2,1,0:T(8,128)(2,1)}, u32[]{:S(2)}) copy-start(bf16[1,3584,512]{2,1,0:T(8,128)(2,1)} %param.12) | copy-start | bytes 11010052
  35.9 5.8 %collective-permute-start.10 = (bf16[128,3712]{1,0:T(8,128)(2,1)S(1)}, bf16[128,3712]{1,0:T(8,128)(2,1)S(1)}, u32[]{:S(2)}, u32[]{:S(2)}) collective-permute-start(bf16[128,3712]{1,0:T(8,128)(2,1)S(1)} %pad_maximum_fusion), channel_id=1, source_target_pairs={{0,2},{1,3},{2,0},{3,1},{4,6},{5,7},{6,4},{7,5},{8,10},{9,11},{10,... | collective-permute-start | bytes 2850824 | tf_op jit(solution)/shard_map/rows_1_core/ppermute | solution.py:110
  36.1 3.1 %copy-start.3 = (bf16[8,3712]{1,0:T(8,128)(2,1)}, bf16[8,3712]{1,0:T(8,128)(2,1)S(1)}, u32[]{:S(2)}) copy-start(bf16[8,3712]{1,0:T(8,128)(2,1)S(1)} %slice_select_fusion.2) | copy-start | bytes 178180
  38.0 2.9 %copy-start = (bf16[1,1024,1792]{2,1,0:T(8,128)(2,1)S(1)}, bf16[1,1024,1792]{2,1,0:T(8,128)(2,1)}, u32[]{:S(2)}) copy-start(bf16[1,1024,1792]{2,1,0:T(8,128)(2,1)} %param.13) | copy-start | bytes 11010052
  39.3 9.1 %collective-permute-start.9 = (bf16[256,512]{1,0:T(8,128)(2,1)S(1)}, bf16[256,512]{1,0:T(8,128)(2,1)S(1)}, u32[]{:S(2)}, u32[]{:S(2)}) collective-permute-start(bf16[256,512]{1,0:T(8,128)(2,1)S(1)} %pad_maximum_fusion.3), channel_id=1, source_target_pairs={{0,1},{1,0},{2,3},{3,2},{4,5},{5,4},{6,7},{7,6},{8,9},{9,8},{10,11... | collective-permute-start | bytes 786440 | tf_op jit(solution)/shard_map/acts_0/ppermute | solution.py:110
  43.2 8.9 %collective-permute-start.15 = (bf16[256,512]{1,0:T(8,128)(2,1)S(1)}, bf16[256,512]{1,0:T(8,128)(2,1)S(1)}, u32[]{:S(2)}, u32[]{:S(2)}) collective-permute-start(bf16[256,512]{1,0:T(8,128)(2,1)S(1)} %pad_maximum_fusion.4), channel_id=1, source_target_pairs={{0,1},{1,0},{2,3},{3,2},{4,5},{5,4},{6,7},{7,6},{8,9},{9,8},{10,11... | collective-permute-start | bytes 786440 | tf_op jit(solution)/shard_map/acts_1/ppermute | solution.py:110
  48.9 3.7 %collective-permute-start.11 = (bf16[128,1792]{1,0:T(8,128)(2,1)S(1)}, bf16[128,1792]{1,0:T(8,128)(2,1)S(1)}, u32[]{:S(2)}, u32[]{:S(2)}) collective-permute-start(bf16[128,1792]{1,0:T(8,128)(2,1)S(1)} %fusion.11), channel_id=1, source_target_pairs={{0,2},{1,3},{2,0},{3,1},{4,6},{5,7},{6,4},{7,5},{8,10},{9,11},{10,... | collective-permute-start | bytes 1376264 | tf_op jit(solution)/shard_map/sums_0_core/ppermute | solution.py:110
  52.5 2.5 %collective-permute-start.16 = (bf16[128,1792]{1,0:T(8,128)(2,1)S(1)}, bf16[128,1792]{1,0:T(8,128)(2,1)S(1)}, u32[]{:S(2)}, u32[]{:S(2)}) collective-permute-start(bf16[128,1792]{1,0:T(8,128)(2,1)S(1)} %fusion.19), channel_id=1, source_target_pairs={{0,2},{1,3},{2,0},{3,1},{4,6},{5,7},{6,4},{7,5},{8,10},{9,11},{10,... | collective-permute-start | bytes 1376264 | tf_op jit(solution)/shard_map/sums_1_core/ppermute | solution.py:110
  53.3 6.1 %collective-permute-start.12 = (bf16[64,1792]{1,0:T(8,128)(2,1)S(1)}, bf16[64,1792]{1,0:T(8,128)(2,1)S(1)}, u32[]{:S(2)}, u32[]{:S(2)}) collective-permute-start(bf16[64,1792]{1,0:T(8,128)(2,1)S(1)} %fusion.42), channel_id=1, source_target_pairs={{0,4},{1,5},{2,10},{3,11},{4,0},{5,1},{6,14},{7,15},{8,12},{9,13},... | collective-permute-start | bytes 688136 | tf_op jit(solution)/shard_map/sums_0_0/ppermute | solution.py:110
  55.7 6.2 %collective-permute-start.17 = (bf16[64,1792]{1,0:T(8,128)(2,1)S(1)}, bf16[64,1792]{1,0:T(8,128)(2,1)S(1)}, u32[]{:S(2)}, u32[]{:S(2)}) collective-permute-start(bf16[64,1792]{1,0:T(8,128)(2,1)S(1)} %fusion.44), channel_id=1, source_target_pairs={{0,4},{1,5},{2,10},{3,11},{4,0},{5,1},{6,14},{7,15},{8,12},{9,13},... | collective-permute-start | bytes 688136 | tf_op jit(solution)/shard_map/sums_1_0/ppermute | solution.py:110
  59.5 4.9 %collective-permute-start.13 = (bf16[32,1792]{1,0:T(8,128)(2,1)S(1)}, bf16[32,1792]{1,0:T(8,128)(2,1)S(1)}, u32[]{:S(2)}, u32[]{:S(2)}) collective-permute-start(bf16[32,1792]{1,0:T(8,128)(2,1)S(1)} %bitcast.67), channel_id=1, source_target_pairs={{0,8},{1,9},{2,6},{3,7},{4,12},{5,13},{6,2},{7,3},{8,0},{9,1},{10,... | collective-permute-start | bytes 344072 | tf_op jit(solution)/shard_map/sums_0_1/ppermute | solution.py:110
  61.9 10.9 %copy-start.2 = (bf16[16,3584]{1,0:T(8,128)(2,1)S(1)}, bf16[16,3584]{1,0:T(8,128)(2,1)}, u32[]{:S(2)}) copy-start(bf16[16,3584]{1,0:T(8,128)(2,1)} %param.9) | copy-start | bytes 344068
  61.9 10.9 %slice-start = ((bf16[8,3712]{1,0:T(8,128)(2,1)}), bf16[8,3584]{1,0:T(8,128)(2,1)S(1)}, s32[]{:S(2)}) async-start(bf16[8,3712]{1,0:T(8,128)(2,1)} %copy-done.3), calls=%async_computation | async-start | bytes 114688 | tf_op jit(solution)/shard_map/slice | solution.py:270
  62.0 15.8 %copy-start.4 = (bf16[8,3712]{1,0:T(8,128)(2,1)S(1)}, bf16[8,3712]{1,0:T(8,128)(2,1)}, u32[]{:S(2)}) copy-start(bf16[8,3712]{1,0:T(8,128)(2,1)} %copy-done.3) | copy-start | bytes 178180
  62.0 5.5 %collective-permute-start.18 = (bf16[32,1792]{1,0:T(8,128)(2,1)S(1)}, bf16[32,1792]{1,0:T(8,128)(2,1)S(1)}, u32[]{:S(2)}, u32[]{:S(2)}) collective-permute-start(bf16[32,1792]{1,0:T(8,128)(2,1)S(1)} %bitcast.68), channel_id=1, source_target_pairs={{0,8},{1,9},{2,6},{3,7},{4,12},{5,13},{6,2},{7,3},{8,0},{9,1},{10,... | collective-permute-start | bytes 344072 | tf_op jit(solution)/shard_map/sums_1_1/ppermute | solution.py:110
  64.4 13.8 %copy-start.6 = (f32[3584]{0:T(1024)S(1)}, f32[3584]{0:T(1024)}, u32[]{:S(2)}) copy-start(f32[3584]{0:T(1024)} %param.17) | copy-start | bytes 43012
  64.4 6.2 %collective-permute-start.14 = (bf16[16,1792]{1,0:T(8,128)(2,1)S(1)}, bf16[16,1792]{1,0:T(8,128)(2,1)S(1)}, u32[]{:S(2)}, u32[]{:S(2)}) collective-permute-start(bf16[16,1792]{1,0:T(8,128)(2,1)S(1)} %fusion.71), channel_id=1, source_target_pairs={{0,16},{1,17},{2,18},{3,19},{4,20},{5,21},{6,22},{7,23},{8,24},{9,... | collective-permute-start | bytes 172040 | tf_op jit(solution)/shard_map/sums_0_2/ppermute | solution.py:110
  67.5 5.2 %collective-permute-start.19 = (bf16[16,1792]{1,0:T(8,128)(2,1)S(1)}, bf16[16,1792]{1,0:T(8,128)(2,1)S(1)}, u32[]{:S(2)}, u32[]{:S(2)}) collective-permute-start(bf16[16,1792]{1,0:T(8,128)(2,1)S(1)} %fusion.72), channel_id=1, source_target_pairs={{0,16},{1,17},{2,18},{3,19},{4,20},{5,21},{6,22},{7,23},{8,24},{9,... | collective-permute-start | bytes 172040 | tf_op jit(solution)/shard_map/sums_1_2/ppermute | solution.py:110
  72.8 4.9 %collective-permute-start.20 = (bf16[32,1792]{1,0:T(8,128)(2,1)S(1)}, bf16[32,1792]{1,0:T(8,128)(2,1)S(1)}, u32[]{:S(2)}, u32[]{:S(2)}) collective-permute-start(bf16[32,1792]{1,0:T(8,128)(2,1)S(1)} %fusion.45), channel_id=1, source_target_pairs={{0,1},{1,0},{2,3},{3,2},{4,5},{5,4},{6,7},{7,6},{8,9},{9,8},{10,11... | collective-permute-start | bytes 344072 | tf_op jit(solution)/shard_map/layer/ppermute | solution.py:110
  77.8 1.1 %copy-start.1 = (bf16[16,3584]{1,0:T(8,128)(2,1)}, bf16[16,3584]{1,0:T(8,128)(2,1)S(1)}, u32[]{:S(2)}) copy-start(bf16[16,3584]{1,0:T(8,128)(2,1)S(1)} %slice.621) | copy-start | bytes 344068
